TPU v7x, 32 devices: a whole 2x2x4 slice. The times are simulated.
32 devices in a mesh: seq: 8 (over z, y), head: 4 (over x, core).
Axes of the slice: x: 2, y: 2, z: 4, core: 2. Of those that a mesh axis runs over, the one named last changes fastest.
Arguments:
- query: bfloat16 [2048, 512], P('seq', 'head'), may hold values from -131 to 131
- keys: bfloat16 [2048, 512], P('seq', 'head'), may hold values from -5 to 5, as said below
- values: bfloat16 [2048, 512], P('seq', 'head'), may hold values from -5 to 5, as said below
- d_out: bfloat16 [2048, 5376], P('seq', 'head'), may hold values from -6 to 6
- w_out: bfloat16 [512, 5376], P('head'), may hold values from -0.25 to 0.25
- w_query: bfloat16 [5376, 512], P(None, 'head'), may hold values from -0.078125 to 0.078125
- w_key: bfloat16 [5376, 512], P(None, 'head'), as said below
- w_value: bfloat16 [5376, 512], P(None, 'head'), as said below
Outputs:
- grad_input: bfloat16 [2048, 5376], P('seq', 'head')
Inputs may be any that keep to these rules, and one draw needn't show every extreme that they name: `keys`: the columns of query heads 2i and 2i + 1 are equal: both read key head i. `values`: the columns of query heads 2i and 2i + 1 are equal: both read value head i. `w_key`: the columns of query heads 2i and 2i + 1 are equal; every entry lies within 5 / sqrt(5376) in magnitude. `w_value`: the columns of query heads 2i and 2i + 1 are equal; every entry lies within 5 / sqrt(5376) in magnitude.
All inputs are finite; a program needn't handle non-finite values.
Results may differ from a plain program's by a relative error of at most 0.03.
Values may be sent and summed in bfloat16 or wider, within the bound.
A program may use at most 64 MiB of HBM per device.

v0:
```python
import jax
import jax.numpy as jnp
from jax import lax
from jax.sharding import PartitionSpec as P

WINDOW = 1024
NBR = 4


score_scale = 168.0 ** (-0.5)


def from_behind(block, axis, distance):
    devices = range(lax.axis_size(axis))
    route = [(i - distance, i) for i in devices if i - distance in devices]
    return lax.ppermute(block, axis, route)


def dot_rows(left, right):
    return lax.dot_general(
        left, right, (((1,), (1,)), ((), ())), preferred_element_type=jnp.float32
    )


def dot_cols(left, right):
    return lax.dot_general(
        left, right, (((0,), (0,)), ((), ())), preferred_element_type=jnp.float32
    )


def band_backward(query_block, key_band, value_band, grad_block, query_start, key_start):
    length = query_block.shape[0]
    span = key_band.shape[0]
    query_pos = query_start + jnp.arange(length, dtype=jnp.int32)
    key_pos = key_start + jnp.arange(span, dtype=jnp.int32)
    offset = query_pos[:, None] - key_pos[None, :]
    allowed = (key_pos[None, :] >= 0) & (offset >= 0) & (offset < WINDOW)
    scores = dot_rows(query_block, key_band) * score_scale
    masked = jnp.where(allowed, scores, -1e30)
    top = jnp.max(masked, axis=1, keepdims=True)
    weights = jnp.where(allowed, jnp.exp(masked - top), 0.0)
    probs = weights / jnp.sum(weights, axis=1, keepdims=True)
    probs_low = probs.astype(jnp.bfloat16)
    grad_probs = dot_rows(grad_block, value_band)
    delta = jnp.sum(probs * grad_probs, axis=1, keepdims=True)
    grad_scores = (probs * (grad_probs - delta)).astype(jnp.bfloat16)
    grad_query = (
        jnp.dot(grad_scores, key_band, preferred_element_type=jnp.float32) * score_scale
    ).astype(jnp.bfloat16)
    grad_keys = (dot_cols(grad_scores, query_block) * score_scale).astype(jnp.bfloat16)
    grad_values = dot_cols(probs_low, grad_block).astype(jnp.bfloat16)
    return (grad_query, grad_keys, grad_values)


def body(query, keys, values, d_out, w_out, w_query, w_key, w_value):
    length = query.shape[0]
    seq_index = lax.axis_index("seq")
    gathered = lax.all_gather(d_out, "head", axis=1, tiled=True)
    grad_heads = dot_rows(gathered, w_out).astype(jnp.bfloat16)
    reach = NBR
    key_blocks = []
    value_blocks = []
    for distance in range(reach, 0, -1):
        far_keys, far_values = from_behind((keys, values), "seq", distance)
        key_blocks.append(far_keys)
        value_blocks.append(far_values)
    key_band = jnp.concatenate(key_blocks + [keys], axis=0)
    value_band = jnp.concatenate(value_blocks + [values], axis=0)
    query_start = seq_index * length
    grad_query, key_parts, value_parts = band_backward(
        query, key_band, value_band, grad_heads, query_start, query_start - reach * length
    )
    key_total = key_parts[reach * length :].astype(jnp.float32)
    value_total = value_parts[reach * length :].astype(jnp.float32)
    for distance in range(1, reach + 1):
        first = (reach - distance) * length
        outgoing = (key_parts[first : first + length], value_parts[first : first + length])
        back_keys, back_values = from_behind((outgoing[0], outgoing[1]), "seq", -distance)
        key_total = key_total + back_keys.astype(jnp.float32)
        value_total = value_total + back_values.astype(jnp.float32)
    grad_keys = key_total.astype(jnp.bfloat16)
    grad_values = value_total.astype(jnp.bfloat16)
    summed = dot_rows(w_query, grad_query)
    summed = summed + dot_rows(w_key, grad_keys)
    summed = summed + dot_rows(w_value, grad_values)
    reduced = lax.psum_scatter(
        summed.astype(jnp.bfloat16), "head", scatter_dimension=0, tiled=True
    ).astype(jnp.float32)
    return reduced.T.astype(jnp.bfloat16)


def solution(mesh):
    in_specs = (
        P("seq", "head"),
        P("seq", "head"),
        P("seq", "head"),
        P("seq", "head"),
        P("head", None),
        P(None, "head"),
        P(None, "head"),
        P(None, "head"),
    )
    out_specs = P("seq", "head")
    return jax.shard_map(body, mesh=mesh, in_specs=in_specs, out_specs=out_specs, check_vma=False)
```

profile of v0, /device:TPU:0, one launch (start us, length us, event | category | flops | bytes accessed | tf_op | source)
XLA Modules:
  0.0 132.7 jit_solution(4567988113010745550)
XLA Ops:
  6.5 0.0 copy-start
  6.5 0.0 all-gather.2.cloned.1.call-start
  6.5 0.7 all-gather.2.cloned.1.call-update
  7.3 0.0 reduce-scatter.4.cloned.1.call-start
  7.3 4.9 %collective-permute-start.2 = (bf16[256,128]{1,0:T(8,128)(2,1)}, bf16[256,128]{1,0:T(8,128)(2,1)S(1)}, u32[]{:S(2)}, u32[]{:S(2)}) collective-permute-start(bf16[256,128]{1,0:T(8,128)(2,1)} %param.9), channel_id=1, source_target_pairs={{0,8},{4,12},{8,16},{12,20},{16,24},{20,28},{1,9},{5,13},{9,17},{1... | collective-permute-start | bytes 196616 | tf_op jit(solution)/shard_map/ppermute | solution.py:16
  12.2 4.4 %collective-permute-start.1 = (bf16[256,128]{1,0:T(8,128)(2,1)}, bf16[256,128]{1,0:T(8,128)(2,1)S(1)}, u32[]{:S(2)}, u32[]{:S(2)}) collective-permute-start(bf16[256,128]{1,0:T(8,128)(2,1)} %param.9), channel_id=1, source_target_pairs={{0,12},{4,16},{8,20},{12,24},{16,28},{1,13},{5,17},{9,21},{13,25},... | collective-permute-start | bytes 196616 | tf_op jit(solution)/shard_map/ppermute | solution.py:16
  16.7 2.3 %collective-permute-start = (bf16[256,128]{1,0:T(8,128)(2,1)}, bf16[256,128]{1,0:T(8,128)(2,1)S(1)}, u32[]{:S(2)}, u32[]{:S(2)}) collective-permute-start(bf16[256,128]{1,0:T(8,128)(2,1)} %param.9), channel_id=1, source_target_pairs={{0,16},{4,20},{8,24},{12,28},{1,17},{5,21},{9,25},{13,29},{2,18},{... | collective-permute-start | bytes 196616 | tf_op jit(solution)/shard_map/ppermute | solution.py:16
  19.0 2.5 %collective-permute-start.3 = (bf16[256,128]{1,0:T(8,128)(2,1)}, bf16[256,128]{1,0:T(8,128)(2,1)S(1)}, u32[]{:S(2)}, u32[]{:S(2)}) collective-permute-start(bf16[256,128]{1,0:T(8,128)(2,1)} %param.9), channel_id=1, source_target_pairs={{0,4},{4,8},{8,12},{12,16},{16,20},{20,24},{24,28},{1,5},{5,9},{9,... | collective-permute-start | bytes 196616 | tf_op jit(solution)/shard_map/ppermute | solution.py:16
  21.5 1.3 collective-permute-start.4
  22.8 2.2 %collective-permute-done.4 = bf16[256,128]{1,0:T(8,128)(2,1)S(1)} collective-permute-done((bf16[256,128]{1,0:T(8,128)(2,1)}, bf16[256,128]{1,0:T(8,128)(2,1)S(1)}, u32[]{:S(2)}, u32[]{:S(2)}) %collective-permute-start.4) | collective-permute-done | bytes 65568 | tf_op jit(solution)/shard_map/ppermute | solution.py:16
  25.0 4.5 %collective-permute-start.5 = (bf16[256,128]{1,0:T(8,128)(2,1)}, bf16[256,128]{1,0:T(8,128)(2,1)S(1)}, u32[]{:S(2)}, u32[]{:S(2)}) collective-permute-start(bf16[256,128]{1,0:T(8,128)(2,1)} %param.10), channel_id=1, source_target_pairs={{0,12},{4,16},{8,20},{12,24},{16,28},{1,13},{5,17},{9,21},{13,25},... | collective-permute-start | bytes 196616 | tf_op jit(solution)/shard_map/ppermute | solution.py:16
  29.5 2.2 %collective-permute-done.5 = bf16[256,128]{1,0:T(8,128)(2,1)S(1)} collective-permute-done((bf16[256,128]{1,0:T(8,128)(2,1)}, bf16[256,128]{1,0:T(8,128)(2,1)S(1)}, u32[]{:S(2)}, u32[]{:S(2)}) %collective-permute-start.5) | collective-permute-done | bytes 65568 | tf_op jit(solution)/shard_map/ppermute | solution.py:16
  31.7 4.0 %collective-permute-start.6 = (bf16[256,128]{1,0:T(8,128)(2,1)}, bf16[256,128]{1,0:T(8,128)(2,1)S(1)}, u32[]{:S(2)}, u32[]{:S(2)}) collective-permute-start(bf16[256,128]{1,0:T(8,128)(2,1)} %param.10), channel_id=1, source_target_pairs={{0,8},{4,12},{8,16},{12,20},{16,24},{20,28},{1,9},{5,13},{9,17},{1... | collective-permute-start | bytes 196616 | tf_op jit(solution)/shard_map/ppermute | solution.py:16
  35.7 2.2 %collective-permute-done.6 = bf16[256,128]{1,0:T(8,128)(2,1)S(1)} collective-permute-done((bf16[256,128]{1,0:T(8,128)(2,1)}, bf16[256,128]{1,0:T(8,128)(2,1)S(1)}, u32[]{:S(2)}, u32[]{:S(2)}) %collective-permute-start.6) | collective-permute-done | bytes 65568 | tf_op jit(solution)/shard_map/ppermute | solution.py:16
  37.9 3.5 %collective-permute-start.7 = (bf16[256,128]{1,0:T(8,128)(2,1)}, bf16[256,128]{1,0:T(8,128)(2,1)S(1)}, u32[]{:S(2)}, u32[]{:S(2)}) collective-permute-start(bf16[256,128]{1,0:T(8,128)(2,1)} %param.10), channel_id=1, source_target_pairs={{0,4},{4,8},{8,12},{12,16},{16,20},{20,24},{24,28},{1,5},{5,9},{9,... | collective-permute-start | bytes 196616 | tf_op jit(solution)/shard_map/ppermute | solution.py:16
  41.4 2.2 %collective-permute-done.7 = bf16[256,128]{1,0:T(8,128)(2,1)S(1)} collective-permute-done((bf16[256,128]{1,0:T(8,128)(2,1)}, bf16[256,128]{1,0:T(8,128)(2,1)S(1)}, u32[]{:S(2)}, u32[]{:S(2)}) %collective-permute-start.7) | collective-permute-done | bytes 65568 | tf_op jit(solution)/shard_map/ppermute | solution.py:16
  43.6 0.9 constant_dynamic-update-slice_fusion.5
  44.5 0.0 collective-permute-done
  44.5 0.0 collective-permute-done.1
  44.5 0.0 collective-permute-done.2
  44.6 0.0 collective-permute-done.3
  44.6 0.0 copy-done.6
  44.6 0.0 copy-done.5
  44.6 0.0 copy-start.2
  44.6 0.6 fusion.19
  45.3 0.1 copy-done.2
  45.4 0.9 fusion.10
  46.3 0.0 all-gather.2.cloned.1.call-done
  46.3 3.1 %convolution_convert_fusion.1 = bf16[256,128]{1,0:T(8,128)(2,1)S(1)} fusion(bf16[256,5376]{0,1:T(8,128)(2,1)} %all-gather.2.cloned.1.call-done, bf16[128,5376]{1,0:T(8,128)(2,1)} %param.12), kind=kOutput, calls=%fused_computation.19 | convolution fusion | flops 352354304 | bytes 4194304 | tf_op jit(solution)/shard_map/dot_general | solution.py:20
  49.4 1.2 convolution_convert_fusion
  50.6 0.0 copy-start.4
  50.6 0.7 fusion.17
  51.4 0.0 copy-done.4
  51.4 1.3 collective-permute-start.12
  52.7 0.7 multiply_reduce_fusion
  53.5 1.7 %multiply_convert_fusion = bf16[256,1280]{0,1:T(8,128)(2,1)S(1)} fusion(f32[256,1280]{0,1:T(8,128)S(1)} %get-tuple-element.16, f32[256]{0:T(256)S(1)} %get-tuple-element.15, f32[256]{0:T(256)} %copy-done.10, f32[256,1280]{0,1:T(8,128)S(1)} %get-tuple-element.14, f32[256]{0:T(256)} %copy-done.9, s32[1280]{0:T(1024)S(1)} %iota_add_fusion, ...), kind=kLoop, calls=%fused_computation.12 | loop fusion | flops 3604480 | bytes 3287296 | tf_op jit(solution)/shard_map/convert_element_type | solution.py:46
  55.2 0.0 copy-start.3
  55.2 0.3 fusion.4
  55.6 1.3 collective-permute-start.8
  56.9 1.3 collective-permute-start.11
  58.2 1.3 collective-permute-start.10
  59.5 0.0 copy-start.8
  59.5 0.0 copy-start.7
  59.5 1.4 %collective-permute-start.9 = (bf16[256,128]{1,0:T(8,128)(2,1)S(1)}, bf16[256,128]{1,0:T(8,128)(2,1)S(1)}, u32[]{:S(2)}, u32[]{:S(2)}) collective-permute-start(bf16[256,128]{1,0:T(8,128)(2,1)S(1)} %get-tuple-element.12), channel_id=1, source_target_pairs={{8,0},{12,4},{16,8},{20,12},{24,16},{28,20},{9,1},{13,5},{17,9},{2... | collective-permute-start | bytes 196616 | tf_op jit(solution)/shard_map/ppermute | solution.py:16
  60.9 0.0 copy-done
  60.9 0.0 copy-done.3
  61.0 3.6 %fusion.8 = f32[256,5376]{1,0:T(8,128)} fusion(bf16[5376,128]{1,0:T(8,128)(2,1)S(1)} %copy-done, bf16[256,1280]{0,1:T(8,128)(2,1)S(1)} %multiply_convert_fusion, bf16[1280,128]{1,0:T(8,128)(2,1)S(1)} %copy-done.3), kind=kOutput, calls=%fused_computation.20 | convolution fusion | flops 436273152 | bytes 7864320 | tf_op jit(solution)/shard_map/dot_general | solution.py:20
  64.6 0.0 collective-permute-done.8
  64.6 1.3 collective-permute-start.15
  65.8 3.4 %collective-permute-done.11 = bf16[256,128]{1,0:T(8,128)(2,1)S(1)} collective-permute-done((bf16[256,128]{1,0:T(8,128)(2,1)S(1)}, bf16[256,128]{1,0:T(8,128)(2,1)S(1)}, u32[]{:S(2)}, u32[]{:S(2)}) %collective-permute-start.11) | collective-permute-done | bytes 65568 | tf_op jit(solution)/shard_map/ppermute | solution.py:16
  69.2 1.3 collective-permute-start.14
  70.5 0.0 collective-permute-done.10
  70.5 0.0 copy-start.1
  70.5 1.4 %collective-permute-start.13 = (bf16[256,128]{1,0:T(8,128)(2,1)S(1)}, bf16[256,128]{1,0:T(8,128)(2,1)S(1)}, u32[]{:S(2)}, u32[]{:S(2)}) collective-permute-start(bf16[256,128]{1,0:T(8,128)(2,1)S(1)} %get-tuple-element.8), channel_id=1, source_target_pairs={{8,0},{12,4},{16,8},{20,12},{24,16},{28,20},{9,1},{13,5},{17,9},{2... | collective-permute-start | bytes 196616 | tf_op jit(solution)/shard_map/ppermute | solution.py:16
  72.0 0.0 collective-permute-done.9
  72.0 3.9 %convolution_add_fusion.1 = f32[256,5376]{1,0:T(8,128)S(1)} fusion(f32[256,5376]{1,0:T(8,128)} %fusion.8, bf16[5376,128]{1,0:T(8,128)(2,1)} %param.14, bf16[256,128]{1,0:T(8,128)(2,1)S(1)} %collective-permute-done.11, bf16[256,128]{1,0:T(8,128)(2,1)S(1)} %collective-permute-done.10, bf16[256,128]{1,0:T(8,128)(2,1)S(1)} %collective-permute-done.9, ...), kind=kOutput, calls=%fused_computation.1 | convolution fusion | flops 354025472 | bytes 12713984 | tf_op jit(solution)/shard_map/dot_general | solution.py:20
  75.8 0.0 collective-permute-done.12
  75.9 2.4 %collective-permute-done.15 = bf16[256,128]{1,0:T(8,128)(2,1)S(1)} collective-permute-done((bf16[256,128]{1,0:T(8,128)(2,1)S(1)}, bf16[256,128]{1,0:T(8,128)(2,1)S(1)}, u32[]{:S(2)}, u32[]{:S(2)}) %collective-permute-start.15) | collective-permute-done | bytes 65568 | tf_op jit(solution)/shard_map/ppermute | solution.py:16
  78.2 0.6 collective-permute-done.14
  78.8 0.0 collective-permute-done.13
  78.8 3.3 %fusion.1 = bf16[5376,256]{0,1:T(8,128)(2,1)} fusion(f32[256,5376]{1,0:T(8,128)S(1)} %convolution_add_fusion.1, bf16[5376,128]{1,0:T(8,128)(2,1)S(1)} %copy-done.1, bf16[256,128]{1,0:T(8,128)(2,1)S(1)} %collective-permute-done.15, bf16[256,128]{1,0:T(8,128)(2,1)S(1)} %collective-permute-done.14, bf16[256,128]{1,0:T(8,128)(2,1)S(1)} %collective-permute-done.13, ...), kind=kOutput, calls=%fused_computation.3 | convolution fusion | flops 355401728 | bytes 9961472 | tf_op jit(solution)/shard_map/dot_general | solution.py:20
  82.1 4.6 %copy.16 = bf16[5376,256]{1,0:T(8,128)(2,1)} copy(bf16[5376,256]{0,1:T(8,128)(2,1)} %fusion.1) | data formatting | bytes 5505024
  86.7 0.0 reduce-scatter.4.cloned.1.call-update
  86.8 39.1 %reduce-scatter.4.cloned.1.call-done = bf16[1344,256]{1,0:T(8,128)(2,1)} async-done(((bf16[5376,256]{1,0:T(8,128)(2,1)}), bf16[1344,256]{1,0:T(8,128)(2,1)}) %reduce-scatter.4.cloned.1.call-update) | async-done | bytes 688144
  (22 shorter events, 0.2 us)
Async XLA Ops:
  6.5 54.4 %copy-start = (bf16[5376,128]{1,0:T(8,128)(2,1)S(1)}, bf16[5376,128]{1,0:T(8,128)(2,1)}, u32[]{:S(2)}) copy-start(bf16[5376,128]{1,0:T(8,128)(2,1)} %param.13) | copy-start | bytes 4128772
  6.5 38.1 %copy-start.6 = (bf16[256,128]{1,0:T(8,128)(2,1)S(1)}, bf16[256,128]{1,0:T(8,128)(2,1)}, u32[]{:S(2)}) copy-start(bf16[256,128]{1,0:T(8,128)(2,1)} %param.9) | copy-start | bytes 196612
  6.5 38.1 %copy-start.5 = (bf16[256,128]{1,0:T(8,128)(2,1)S(1)}, bf16[256,128]{1,0:T(8,128)(2,1)}, u32[]{:S(2)}) copy-start(bf16[256,128]{1,0:T(8,128)(2,1)} %param.8) | copy-start | bytes 196612
  6.5 39.7 %all-gather.2.cloned.1.call-start = ((), (), s32[]{:S(2)}) async-start(), calls=%async_computation.1 | async-start | bytes 3440640 | tf_op jit(solution)/shard_map/all_gather | solution.py:58
  7.3 118.6 %reduce-scatter.4.cloned.1.call-start = ((), (), s32[]{:S(2)}) async-start(), calls=%async_computation.2 | async-start | bytes 3440640
  7.3 37.2 %collective-permute-start.2 = (bf16[256,128]{1,0:T(8,128)(2,1)}, bf16[256,128]{1,0:T(8,128)(2,1)S(1)}, u32[]{:S(2)}, u32[]{:S(2)}) collective-permute-start(bf16[256,128]{1,0:T(8,128)(2,1)} %param.9), channel_id=1, source_target_pairs={{0,8},{4,12},{8,16},{12,20},{16,24},{20,28},{1,9},{5,13},{9,17},{1... | collective-permute-start | bytes 196616 | tf_op jit(solution)/shard_map/ppermute | solution.py:16
  12.2 32.3 %collective-permute-start.1 = (bf16[256,128]{1,0:T(8,128)(2,1)}, bf16[256,128]{1,0:T(8,128)(2,1)S(1)}, u32[]{:S(2)}, u32[]{:S(2)}) collective-permute-start(bf16[256,128]{1,0:T(8,128)(2,1)} %param.9), channel_id=1, source_target_pairs={{0,12},{4,16},{8,20},{12,24},{16,28},{1,13},{5,17},{9,21},{13,25},... | collective-permute-start | bytes 196616 | tf_op jit(solution)/shard_map/ppermute | solution.py:16
  16.7 27.8 %collective-permute-start = (bf16[256,128]{1,0:T(8,128)(2,1)}, bf16[256,128]{1,0:T(8,128)(2,1)S(1)}, u32[]{:S(2)}, u32[]{:S(2)}) collective-permute-start(bf16[256,128]{1,0:T(8,128)(2,1)} %param.9), channel_id=1, source_target_pairs={{0,16},{4,20},{8,24},{12,28},{1,17},{5,21},{9,25},{13,29},{2,18},{... | collective-permute-start | bytes 196616 | tf_op jit(solution)/shard_map/ppermute | solution.py:16
  19.0 25.6 %collective-permute-start.3 = (bf16[256,128]{1,0:T(8,128)(2,1)}, bf16[256,128]{1,0:T(8,128)(2,1)S(1)}, u32[]{:S(2)}, u32[]{:S(2)}) collective-permute-start(bf16[256,128]{1,0:T(8,128)(2,1)} %param.9), channel_id=1, source_target_pairs={{0,4},{4,8},{8,12},{12,16},{16,20},{20,24},{24,28},{1,5},{5,9},{9,... | collective-permute-start | bytes 196616 | tf_op jit(solution)/shard_map/ppermute | solution.py:16
  21.5 3.5 %collective-permute-start.4 = (bf16[256,128]{1,0:T(8,128)(2,1)}, bf16[256,128]{1,0:T(8,128)(2,1)S(1)}, u32[]{:S(2)}, u32[]{:S(2)}) collective-permute-start(bf16[256,128]{1,0:T(8,128)(2,1)} %param.10), channel_id=1, source_target_pairs={{0,16},{4,20},{8,24},{12,28},{1,17},{5,21},{9,25},{13,29},{2,18},{... | collective-permute-start | bytes 196616 | tf_op jit(solution)/shard_map/ppermute | solution.py:16
  25.0 6.7 %collective-permute-start.5 = (bf16[256,128]{1,0:T(8,128)(2,1)}, bf16[256,128]{1,0:T(8,128)(2,1)S(1)}, u32[]{:S(2)}, u32[]{:S(2)}) collective-permute-start(bf16[256,128]{1,0:T(8,128)(2,1)} %param.10), channel_id=1, source_target_pairs={{0,12},{4,16},{8,20},{12,24},{16,28},{1,13},{5,17},{9,21},{13,25},... | collective-permute-start | bytes 196616 | tf_op jit(solution)/shard_map/ppermute | solution.py:16
  31.7 6.2 %collective-permute-start.6 = (bf16[256,128]{1,0:T(8,128)(2,1)}, bf16[256,128]{1,0:T(8,128)(2,1)S(1)}, u32[]{:S(2)}, u32[]{:S(2)}) collective-permute-start(bf16[256,128]{1,0:T(8,128)(2,1)} %param.10), channel_id=1, source_target_pairs={{0,8},{4,12},{8,16},{12,20},{16,24},{20,28},{1,9},{5,13},{9,17},{1... | collective-permute-start | bytes 196616 | tf_op jit(solution)/shard_map/ppermute | solution.py:16
  37.9 5.7 %collective-permute-start.7 = (bf16[256,128]{1,0:T(8,128)(2,1)}, bf16[256,128]{1,0:T(8,128)(2,1)S(1)}, u32[]{:S(2)}, u32[]{:S(2)}) collective-permute-start(bf16[256,128]{1,0:T(8,128)(2,1)} %param.10), channel_id=1, source_target_pairs={{0,4},{4,8},{8,12},{12,16},{16,20},{20,24},{24,28},{1,5},{5,9},{9,... | collective-permute-start | bytes 196616 | tf_op jit(solution)/shard_map/ppermute | solution.py:16
  44.6 0.7 copy-start.2
  45.4 7.3 %copy-start.9 = (f32[256]{0:T(256)}, f32[256]{0:T(256)S(1)}, u32[]{:S(2)}) copy-start(f32[256]{0:T(256)S(1)} %get-tuple-element.13) | copy-start | bytes 3076
  46.3 6.4 %copy-start.10 = (f32[256]{0:T(256)}, f32[256]{0:T(256)S(1)}, u32[]{:S(2)}) copy-start(f32[256]{0:T(256)S(1)} %fusion.10) | copy-start | bytes 3076
  50.6 0.8 copy-start.4
  51.4 24.4 %collective-permute-start.12 = (bf16[256,128]{1,0:T(8,128)(2,1)}, bf16[256,128]{1,0:T(8,128)(2,1)S(1)}, u32[]{:S(2)}, u32[]{:S(2)}) collective-permute-start(bf16[256,128]{1,0:T(8,128)(2,1)} %get-tuple-element.5), channel_id=1, source_target_pairs={{4,0},{8,4},{12,8},{16,12},{20,16},{24,20},{28,24},{5,1},{9,5},{13... | collective-permute-start | bytes 196616 | tf_op jit(solution)/shard_map/ppermute | solution.py:16
  55.2 5.7 %copy-start.3 = (bf16[1280,128]{1,0:T(8,128)(2,1)S(1)}, bf16[1280,128]{1,0:T(8,128)(2,1)}, u32[]{:S(2)}) copy-start(bf16[1280,128]{1,0:T(8,128)(2,1)} %copy-done.2) | copy-start | bytes 983044
  55.6 9.0 %collective-permute-start.8 = (bf16[256,128]{1,0:T(8,128)(2,1)S(1)}, bf16[256,128]{1,0:T(8,128)(2,1)S(1)}, u32[]{:S(2)}, u32[]{:S(2)}) collective-permute-start(bf16[256,128]{1,0:T(8,128)(2,1)S(1)} %get-tuple-element.9), channel_id=1, source_target_pairs={{4,0},{8,4},{12,8},{16,12},{20,16},{24,20},{28,24},{5,1},{9,5},{13... | collective-permute-start | bytes 196616 | tf_op jit(solution)/shard_map/ppermute | solution.py:16
  56.9 12.3 %collective-permute-start.11 = (bf16[256,128]{1,0:T(8,128)(2,1)S(1)}, bf16[256,128]{1,0:T(8,128)(2,1)S(1)}, u32[]{:S(2)}, u32[]{:S(2)}) collective-permute-start(bf16[256,128]{1,0:T(8,128)(2,1)S(1)} %get-tuple-element.10), channel_id=1, source_target_pairs={{16,0},{20,4},{24,8},{28,12},{17,1},{21,5},{25,9},{29,13},{18,2},{... | collective-permute-start | bytes 196616 | tf_op jit(solution)/shard_map/ppermute | solution.py:16
  58.2 12.3 %collective-permute-start.10 = (bf16[256,128]{1,0:T(8,128)(2,1)S(1)}, bf16[256,128]{1,0:T(8,128)(2,1)S(1)}, u32[]{:S(2)}, u32[]{:S(2)}) collective-permute-start(bf16[256,128]{1,0:T(8,128)(2,1)S(1)} %get-tuple-element.11), channel_id=1, source_target_pairs={{12,0},{16,4},{20,8},{24,12},{28,16},{13,1},{17,5},{21,9},{25,13},... | collective-permute-start | bytes 196616 | tf_op jit(solution)/shard_map/ppermute | solution.py:16
  59.5 5.1 %copy-start.8 = (bf16[256,128]{1,0:T(8,128)(2,1)S(1)}, bf16[256,128]{1,0:T(8,128)(2,1)}, u32[]{:S(2)}) copy-start(bf16[256,128]{1,0:T(8,128)(2,1)} %get-tuple-element.6) | copy-start | bytes 196612
  59.5 9.7 %copy-start.7 = (bf16[256,128]{1,0:T(8,128)(2,1)S(1)}, bf16[256,128]{1,0:T(8,128)(2,1)}, u32[]{:S(2)}) copy-start(bf16[256,128]{1,0:T(8,128)(2,1)} %get-tuple-element.7) | copy-start | bytes 196612
  59.5 12.5 %collective-permute-start.9 = (bf16[256,128]{1,0:T(8,128)(2,1)S(1)}, bf16[256,128]{1,0:T(8,128)(2,1)S(1)}, u32[]{:S(2)}, u32[]{:S(2)}) collective-permute-start(bf16[256,128]{1,0:T(8,128)(2,1)S(1)} %get-tuple-element.12), channel_id=1, source_target_pairs={{8,0},{12,4},{16,8},{20,12},{24,16},{28,20},{9,1},{13,5},{17,9},{2... | collective-permute-start | bytes 196616 | tf_op jit(solution)/shard_map/ppermute | solution.py:16
  64.6 13.7 %collective-permute-start.15 = (bf16[256,128]{1,0:T(8,128)(2,1)S(1)}, bf16[256,128]{1,0:T(8,128)(2,1)S(1)}, u32[]{:S(2)}, u32[]{:S(2)}) collective-permute-start(bf16[256,128]{1,0:T(8,128)(2,1)S(1)} %copy-done.8), channel_id=1, source_target_pairs={{16,0},{20,4},{24,8},{28,12},{17,1},{21,5},{25,9},{29,13},{18,2},{... | collective-permute-start | bytes 196616 | tf_op jit(solution)/shard_map/ppermute | solution.py:16
  69.2 9.6 %collective-permute-start.14 = (bf16[256,128]{1,0:T(8,128)(2,1)S(1)}, bf16[256,128]{1,0:T(8,128)(2,1)S(1)}, u32[]{:S(2)}, u32[]{:S(2)}) collective-permute-start(bf16[256,128]{1,0:T(8,128)(2,1)S(1)} %copy-done.7), channel_id=1, source_target_pairs={{12,0},{16,4},{20,8},{24,12},{28,16},{13,1},{17,5},{21,9},{25,13},... | collective-permute-start | bytes 196616 | tf_op jit(solution)/shard_map/ppermute | solution.py:16
  70.5 8.3 %copy-start.1 = (bf16[5376,128]{1,0:T(8,128)(2,1)S(1)}, bf16[5376,128]{1,0:T(8,128)(2,1)}, u32[]{:S(2)}) copy-start(bf16[5376,128]{1,0:T(8,128)(2,1)} %param.15) | copy-start | bytes 4128772
  70.5 8.3 %collective-permute-start.13 = (bf16[256,128]{1,0:T(8,128)(2,1)S(1)}, bf16[256,128]{1,0:T(8,128)(2,1)S(1)}, u32[]{:S(2)}, u32[]{:S(2)}) collective-permute-start(bf16[256,128]{1,0:T(8,128)(2,1)S(1)} %get-tuple-element.8), channel_id=1, source_target_pairs={{8,0},{12,4},{16,8},{20,12},{24,16},{28,20},{9,1},{13,5},{17,9},{2... | collective-permute-start | bytes 196616 | tf_op jit(solution)/shard_map/ppermute | solution.py:16
Sparse Core Ops, SparseCore 0:
  8.9 28.9 all-gather.1
  86.9 38.8 reduce-scatter.3
where the time goes:
time: 133 us
  waiting for transfers between devices  54.9 us (41%)
  starting transfers between devices  38 us (29%)
  matrix products  16.7 us (13%)
  between operations  13.8 us (10%)
  local copies, waits for them, and re-layouts  6.53 us (5%)
  other arithmetic  2.66 us (2%)
    unnamed x3, waiting for transfers between devices  39.8 us
    ppermute x16, starting transfers between devices, from_behind(): return lax.ppermute(block, axis, route)  38 us
    dot_general x6, matrix products, dot_rows(): lax.dot_general(left, right, (((1,), (1,)), ((), ())), preferred_element_...  15.2 us
    ppermute x16, waiting for transfers between devices, from_behind(): return lax.ppermute(block, axis, route)  15.1 us
    unnamed x31, local copies, waits for them, and re-layouts  4.91 us
  transfers between devices with their start and end apart: 18, of which 8 were waited for; matrix products, arithmetic and copies ran while one was open for 10% of the time, Pallas kernels for 0%

commit v1 on v0

--- a/solution.py
+++ b/solution.py
@@ -1,10 +1,15 @@
+import functools
+
 import jax
 import jax.numpy as jnp
 from jax import lax
+from jax.experimental import pallas as pl
+from jax.experimental.pallas import tpu as pltpu
 from jax.sharding import PartitionSpec as P
 
 WINDOW = 1024
 NBR = 4
+HEAD = 128
 
 
 score_scale = 168.0 ** (-0.5)
@@ -89,6 +94,388 @@
     return reduced.T.astype(jnp.bfloat16)
 
 
+PEERS = 4
+SIB, ACROSS, DIAG = 1, 2, 3
+ROW_CHUNKS = 4
+MESH = pl.DeviceIdType.MESH
+
+C_DOUT = 0
+C_WOUT = C_DOUT + ROW_CHUNKS
+C_HALO = C_WOUT + 2
+C_PASS = C_HALO + NBR
+C_PART = C_PASS + NBR
+C_WSIB = C_PART + 1
+C_WFAR = C_WSIB + 2
+C_WFWD = C_WFAR + 4
+C_SWAP = C_WFWD + 4
+C_BACK = C_SWAP + 1
+C_GRAD = C_BACK + NBR
+C_END = C_GRAD + 6
+
+
+def kernel(
+    seqs, query, keys, values, d_out, w_out, w_query, w_key, w_value, out,
+    wq_all, wkv_all, w_cut, w_own, w_sib, d_own, d_far, kv, probs, low, ds, partial, partial_in, heads,
+    parts, parts_in, back, back_in, grads, weights, total,
+    send, recv, local,
+):
+    s = lax.axis_index("seq")
+    h = lax.axis_index("head")
+    core = lax.rem(h, 2)
+    sib = h + 1 - 2 * core
+    across = lax.rem(h + 2, 4)
+    diag = lax.rem(sib + 2, 4)
+    y = lax.rem(s, 2)
+    pair = s + 1 - 2 * y
+    peers = (None, sib, across, diag)
+    tokens = query.shape[0]
+    width = out.shape[1]
+    half = width // 2
+    reach = NBR
+    f32, bf16 = jnp.float32, jnp.bfloat16
+
+    def remote(index, src, dst, seq, head):
+        return pltpu.make_async_remote_copy(
+            src_ref=src, dst_ref=dst, send_sem=send.at[index], recv_sem=recv.at[index],
+            device_id=(seq, head), device_id_type=MESH,
+        )
+
+    load_wq = pltpu.make_async_copy(w_query, wq_all, local.at[0])
+    load_wk = pltpu.make_async_copy(w_key, wkv_all, local.at[1])
+    load_wv = pltpu.make_async_copy(w_value, wkv_all, local.at[1])
+    load_wq.start()
+
+    @pl.when(core == 0)
+    def _():
+        load_wk.start()
+
+    @pl.when(core == 1)
+    def _():
+        load_wv.start()
+
+    wide = d_own.shape[1]
+    pad = jnp.zeros((HEAD, wide - width), bf16)
+    d_own[...] = jnp.concatenate([d_out[...], jnp.zeros((tokens, wide - width), bf16)], axis=1)
+    kv[0, reach] = keys[...]
+    kv[1, reach] = values[...]
+    for d in range(1, reach + 1):
+        @pl.when(s < d)
+        def _():
+            kv[0, reach - d] = jnp.zeros((tokens, HEAD), bf16)
+            kv[1, reach - d] = jnp.zeros((tokens, HEAD), bf16)
+
+    barrier = pltpu.get_barrier_semaphore()
+    for r in range(1, PEERS):
+        pl.semaphore_signal(barrier, inc=1, device_id=(s, peers[r]), device_id_type=MESH)
+    for d in range(1, reach + 1):
+        @pl.when(s >= d)
+        def _():
+            pl.semaphore_signal(barrier, inc=1, device_id=(s - d, h), device_id_type=MESH)
+
+        @pl.when(s + d < seqs)
+        def _():
+            pl.semaphore_signal(barrier, inc=1, device_id=(s + d, h), device_id_type=MESH)
+    behind = jnp.minimum(s, reach)
+    ahead = jnp.minimum(seqs - 1 - s, reach)
+    pl.semaphore_wait(barrier, PEERS - 1 + behind + ahead)
+
+    rows = tokens // ROW_CHUNKS
+    dout_copies = [
+        remote(C_DOUT + i, d_own.at[pl.ds(i * rows, rows)], d_far.at[pl.ds(i * rows, rows)], s, across)
+        for i in range(ROW_CHUNKS)
+    ]
+    for copy in dout_copies:
+        copy.start()
+    halo = [
+        remote(C_HALO + d - 1, kv.at[core, reach], kv.at[core, reach - d], s + d, h)
+        for d in range(1, reach + 1)
+    ]
+    for d in range(1, reach + 1):
+        @pl.when(s + d < seqs)
+        def _():
+            halo[d - 1].start()
+
+    for b in range(PEERS):
+        shift = b * width % 128
+        first = b * width - shift
+        room = min(width + 128, w_out.shape[1] - first)
+        cut = w_out[:, first : first + room][:, shift : shift + width]
+        cut = jnp.concatenate([cut, pad], axis=1)
+        w_cut[b] = cut
+
+        @pl.when(h == b)
+        def _():
+            w_own[0] = cut
+
+        @pl.when(across == b)
+        def _():
+            w_own[1] = cut
+    wout_copies = [
+        remote(C_WOUT, w_cut.at[sib], w_sib.at[0], s, sib),
+        remote(C_WOUT + 1, w_cut.at[diag], w_sib.at[1], s, sib),
+    ]
+    for copy in wout_copies:
+        copy.start()
+
+    passed = [
+        remote(C_PASS + d - 1, kv.at[core, reach - d], kv.at[core, reach - d], s, sib)
+        for d in range(1, reach + 1)
+    ]
+    for d in range(1, reach + 1):
+        @pl.when(s >= d)
+        def _():
+            halo[d - 1].wait_recv()
+            passed[d - 1].start()
+
+    sib_rows = pl.ds(pl.multiple_of(sib * width, 16), width)
+    load_wq.wait()
+    load_wk.wait()
+    own_rows = pl.ds(pl.multiple_of(h * width, 16), width)
+    load_own = [
+        pltpu.make_async_copy(w.at[own_rows], weights.at[t, 0], local.at[2 + t])
+        for t, w in enumerate((wq_all, wkv_all))
+    ]
+    for copy in load_own:
+        copy.start()
+    wsib = [
+        remote(C_WSIB + t, w.at[sib_rows], weights.at[t, SIB], s, sib)
+        for t, w in enumerate((wq_all, wkv_all))
+    ]
+    for copy in wsib:
+        copy.start()
+    for d in range(1, reach + 1):
+        @pl.when(s >= d)
+        def _():
+            passed[d - 1].wait_recv()
+
+    for i in range(ROW_CHUNKS):
+        here = pl.ds(i * rows, rows)
+        row = lax.broadcasted_iota(jnp.int32, (rows, tokens), 0) + i * rows
+        col = lax.broadcasted_iota(jnp.int32, (rows, tokens), 1)
+        scores = []
+        for j in range(reach + 1):
+            score = dot_rows(query[here, :], kv[0, j]) * score_scale
+            if j == reach:
+                score = jnp.where(col <= row, score, -1e30)
+            else:
+                score = jnp.where(s >= reach - j, score, -1e30)
+                if j == 0:
+                    score = jnp.where(col > row, score, -1e30)
+            scores.append(score)
+        top = scores[0]
+        for score in scores[1:]:
+            top = jnp.maximum(top, score)
+        top = jnp.max(top, axis=1, keepdims=True)
+        exps = [jnp.exp(score - top) for score in scores]
+        mass = exps[0]
+        for e in exps[1:]:
+            mass = mass + e
+        inverse = 1.0 / jnp.sum(mass, axis=1, keepdims=True)
+        for j in range(reach + 1):
+            p = exps[j] * inverse
+            probs[here, j * tokens : (j + 1) * tokens] = p
+            low[here, j * tokens : (j + 1) * tokens] = p.astype(bf16)
+
+    for copy in wout_copies:
+        copy.wait_recv()
+    for i in range(ROW_CHUNKS):
+        here = pl.ds(i * rows, rows)
+        heads[here, :] = dot_rows(d_own[here, :], w_own[0])
+        partial[here, :] = dot_rows(d_own[here, :], w_sib[0])
+    for i in range(ROW_CHUNKS):
+        here = pl.ds(i * rows, rows)
+        dout_copies[i].wait_recv()
+        partial[here, :] += dot_rows(d_far[here, :], w_sib[1])
+        heads[here, :] += dot_rows(d_far[here, :], w_own[1])
+    part = remote(C_PART, partial, partial_in, s, sib)
+    part.start()
+
+    wfar = []
+    for n, (slot, peer) in enumerate(((ACROSS, across), (DIAG, diag))):
+        src = pl.ds(pl.multiple_of(peer * width + y * half, 16), half)
+        dst = pl.ds(pl.multiple_of(y * half, 16), half)
+        wfar.append([
+            remote(C_WFAR + 2 * t + n, w.at[src], weights.at[t, slot, dst], s, peer)
+            for t, w in enumerate((wq_all, wkv_all))
+        ])
+    for copy in dout_copies:
+        copy.wait_send()
+    for t in range(2):
+        for far in wfar:
+            far[t].start()
+
+    def forward(t, n):
+        slot = (ACROSS, DIAG)[n]
+        mine = pl.ds(pl.multiple_of(y * half, 16), half)
+        block = weights.at[t, slot, mine]
+        return remote(C_WFWD + 2 * t + n, block, block, pair, h)
+
+    def relay(t):
+        for n in range(2):
+            wfar[n][t].wait_recv()
+            forward(t, n).start()
+
+    part.wait_recv()
+    grad_heads = (heads[...] + partial_in[...]).astype(bf16)
+
+    for j in range(reach + 1):
+        parts[1, j] = dot_cols(low[:, j * tokens : (j + 1) * tokens], grad_heads).astype(bf16)
+    swap = remote(C_SWAP, parts.at[1 - core], parts_in, s, sib)
+
+    @pl.when(core == 0)
+    def _():
+        swap.start()
+
+    for i in range(ROW_CHUNKS):
+        here = pl.ds(i * rows, rows)
+        block = grad_heads[i * rows : (i + 1) * rows]
+        weighted = []
+        products = []
+        for j in range(reach + 1):
+            p = probs[here, j * tokens : (j + 1) * tokens]
+            dp = dot_rows(block, kv[1, j])
+            products.append(dp)
+            weighted.append(p * dp)
+        delta = weighted[0]
+        for w in weighted[1:]:
+            delta = delta + w
+        delta = jnp.sum(delta, axis=1, keepdims=True)
+        for j in range(reach + 1):
+            p = probs[here, j * tokens : (j + 1) * tokens]
+            ds[here, j * tokens : (j + 1) * tokens] = (p * (products[j] - delta)).astype(bf16)
+    for j in range(reach + 1):
+        parts[0, j] = (
+            dot_cols(ds[:, j * tokens : (j + 1) * tokens], query[...]) * score_scale
+        ).astype(bf16)
+
+    @pl.when(core == 1)
+    def _():
+        swap.start()
+
+    grad_query = jnp.zeros((tokens, HEAD), f32)
+    for j in range(reach + 1):
+        grad_query = grad_query + jnp.dot(
+            ds[:, j * tokens : (j + 1) * tokens], kv[0, j], preferred_element_type=f32)
+    grads[0, 0] = (grad_query * score_scale).astype(bf16)
+
+    swap.wait_recv()
+    back_copies = [
+        remote(C_BACK + d - 1, back.at[reach - d], back_in.at[d - 1], s - d, h)
+        for d in range(1, reach + 1)
+    ]
+    for d in range(reach, -1, -1):
+        j = reach - d
+        kept = jnp.where(core == 0, parts[0, j].astype(f32), parts[1, j].astype(f32))
+        both = kept + parts_in[j].astype(f32)
+        if d == 0:
+            total[...] = both
+        else:
+            back[j] = both.astype(bf16)
+
+            @pl.when(s >= d)
+            def _():
+                back_copies[d - 1].start()
+
+    def share(t):
+        return [
+            remote(C_GRAD + 3 * t + r - 1, grads.at[t, 0], grads.at[t, r], s, peers[r])
+            for r in range(1, PEERS)
+        ]
+
+    share_query = share(0)
+    for copy in share_query:
+        copy.start()
+    relay(0)
+    relay(1)
+    for d in range(1, reach + 1):
+        @pl.when(s + d < seqs)
+        def _():
+            back_copies[d - 1].wait_recv()
+            total[...] += back_in[d - 1].astype(f32)
+    grads[1, 0] = total[...].astype(bf16)
+    share_pair = share(1)
+    for copy in share_pair:
+        copy.start()
+
+    for copy in wsib:
+        copy.wait_recv()
+    for copy in load_own:
+        copy.wait()
+    for t in range(2):
+        for n in range(2):
+            forward(t, n).wait_recv()
+    for copy in share_query + share_pair:
+        copy.wait_recv()
+    left = jnp.concatenate([grads[t, r] for t in range(2) for r in range(PEERS)], axis=1)
+    for first in range(0, width, 256):
+        size = min(256, width - first)
+        right = [weights[t, r, first : first + size] for t in range(2) for r in range(PEERS)]
+        acc = dot_rows(left, jnp.concatenate(right, axis=1))
+        out[:, first : first + size] = acc.astype(bf16)
+
+    for copy in wout_copies + share_query + share_pair:
+        copy.wait_send()
+    for copy in (part, wsib[0], wsib[1], swap):
+        copy.wait_send()
+    for t in range(2):
+        for n in range(2):
+            wfar[n][t].wait_send()
+            forward(t, n).wait_send()
+    for d in range(1, reach + 1):
+        @pl.when(s + d < seqs)
+        def _():
+            halo[d - 1].wait_send()
+
+        @pl.when(s >= d)
+        def _():
+            passed[d - 1].wait_send()
+            back_copies[d - 1].wait_send()
+
+
+def fused(seqs, query, keys, values, d_out, w_out, w_query, w_key, w_value):
+    tokens, width = d_out.shape
+    wide = -(-width // 128) * 128
+    span = (NBR + 1) * tokens
+    bf16, f32 = jnp.bfloat16, jnp.float32
+    vmem = pl.BlockSpec(memory_space=pltpu.VMEM)
+    anywhere = pl.BlockSpec(memory_space=pl.ANY)
+    return pl.pallas_call(
+        functools.partial(kernel, seqs),
+        out_shape=jax.ShapeDtypeStruct((tokens, width), bf16),
+        in_specs=[vmem] * 5 + [anywhere] * 3,
+        out_specs=vmem,
+        scratch_shapes=[
+            pltpu.VMEM(w_query.shape, bf16),
+            pltpu.VMEM(w_key.shape, bf16),
+            pltpu.VMEM((PEERS, HEAD, wide), bf16),
+            pltpu.VMEM((2, HEAD, wide), bf16),
+            pltpu.VMEM((2, HEAD, wide), bf16),
+            pltpu.VMEM((tokens, wide), bf16),
+            pltpu.VMEM((tokens, wide), bf16),
+            pltpu.VMEM((2, NBR + 1, tokens, HEAD), bf16),
+            pltpu.VMEM((tokens, span), f32),
+            pltpu.VMEM((tokens, span), bf16),
+            pltpu.VMEM((tokens, span), bf16),
+            pltpu.VMEM((tokens, HEAD), f32),
+            pltpu.VMEM((tokens, HEAD), f32),
+            pltpu.VMEM((tokens, HEAD), f32),
+            pltpu.VMEM((2, NBR + 1, tokens, HEAD), bf16),
+            pltpu.VMEM((NBR + 1, tokens, HEAD), bf16),
+            pltpu.VMEM((NBR, tokens, HEAD), bf16),
+            pltpu.VMEM((NBR, tokens, HEAD), bf16),
+            pltpu.VMEM((2, PEERS, tokens, HEAD), bf16),
+            pltpu.VMEM((2, PEERS, width, HEAD), bf16),
+            pltpu.VMEM((tokens, HEAD), f32),
+            pltpu.SemaphoreType.DMA((C_END,)),
+            pltpu.SemaphoreType.DMA((C_END,)),
+            pltpu.SemaphoreType.DMA((4,)),
+        ],
+        compiler_params=pltpu.CompilerParams(
+            collective_id=0, has_side_effects=True, vmem_limit_bytes=48 * 1024 * 1024,
+        ),
+    )(query, keys, values, d_out, w_out, w_query, w_key, w_value)
+
+
 def solution(mesh):
     in_specs = (
         P("seq", "head"),
@@ -101,4 +488,13 @@
         P(None, "head"),
     )
     out_specs = P("seq", "head")
-    return jax.shard_map(body, mesh=mesh, in_specs=in_specs, out_specs=out_specs, check_vma=False)
+    seqs, peers = mesh.shape["seq"], mesh.shape["head"]
+
+    def local(query, keys, values, d_out, w_out, w_query, w_key, w_value):
+        args = (query, keys, values, d_out, w_out, w_query, w_key, w_value)
+        tokens, width = d_out.shape
+        fits = peers == PEERS and seqs % 2 == 0 and query.shape[1] == HEAD
+        fits = fits and tokens * NBR == WINDOW and width % 32 == 0
+        return fused(seqs, *args) if fits else body(*args)
+
+    return jax.shard_map(local, mesh=mesh, in_specs=in_specs, out_specs=out_specs, check_vma=False)

time: 133 us -> 55.2 us (0.42)
  waiting for transfers between devices: 54.9 us -> 0 us
  Pallas kernels: 0 us -> 46.9 us
  starting transfers between devices: 38 us -> 0 us
  matrix products: 16.7 us -> 0 us
  between operations: 13.8 us -> 0.03 us
  other arithmetic: 2.66 us -> 0 us
    pallas_call x0 -> x1, Pallas kernels: none -> 46.9 us  [fused(): pl.pallas_call(functools.partial(kernel, seqs), out_shape=jax.ShapeDtypeS...]
    unnamed x3 -> x0, waiting for transfers between devices: 39.8 us -> none
    ppermute x16 -> x0, starting transfers between devices: 38 us -> none  [from_behind(): return lax.ppermute(block, axis, route)]
    dot_general x8 -> x0, matrix products: 16.7 us -> none  [the longest x6 15.2 us: dot_rows(): lax.dot_general(left, right, (((1,), (1,)), ((), ())), preferred_element_...]
    ppermute x16 -> x0, waiting for transfers between devices: 15.1 us -> none  [from_behind(): return lax.ppermute(block, axis, route)]
    unnamed x31 -> x13, local copies, waits for them, and re-layouts: 4.91 us -> 6.74 us
    convert_element_type x1 -> x0, other arithmetic: 1.75 us -> none  [band_backward(): grad_scores = (probs * (grad_probs - delta)).astype(jnp.bfloat16)]
  transfers between devices with their start and end apart: 18 -> 0, of which waited for: 8 -> 0; matrix products, arithmetic and copies ran while one was open for 10% -> 0% of each run, Pallas kernels for 0% -> 0%
where the time goes in v1:
time: 55.2 us; the launch traced here: 54.8 us
  Pallas kernels  46.9 us (85%)
  local copies, waits for them, and re-layouts  7.85 us (14%)
    pallas_call x1, Pallas kernels, fused(): pl.pallas_call(functools.partial(kernel, seqs), out_shape=jax.ShapeDtypeS...  46.9 us
    unnamed x13, local copies, waits for them, and re-layouts  6.74 us
    pallas_call x1, local copies, waits for them, and re-layouts, fused(): pl.pallas_call(functools.partial(kernel, seqs), out_shape=jax.ShapeDtypeS...  1.11 us

profile of v1, /device:TPU:0, one launch (start us, length us, event | category | flops | bytes accessed | tf_op | source)
XLA Modules:
  0.0 54.8 jit_solution(6811837710858563369)
XLA Ops:
  0.0 0.0 copy-start
  0.0 1.5 %copy.9.d_out = bf16[256,1344]{1,0:T(8,128)(2,1)S(1)} copy(bf16[256,1344]{0,1:T(8,128)(2,1)} %param.11) | data formatting | bytes 1376256 | tf_op args[3]
  1.5 0.0 copy-done
  1.6 0.0 copy-start.1
  1.6 1.3 %copy-done.1 = bf16[5376,128]{1,0:T(8,128)(2,1)S(1)} copy-done((bf16[5376,128]{1,0:T(8,128)(2,1)S(1)}, bf16[5376,128]{1,0:T(8,128)(2,1)}, u32[]{:S(2)}) %copy-start.1) | copy-done | bytes 1376280
  2.9 0.0 copy-start.2
  2.9 1.3 %copy-done.2 = bf16[5376,128]{1,0:T(8,128)(2,1)S(1)} copy-done((bf16[5376,128]{1,0:T(8,128)(2,1)S(1)}, bf16[5376,128]{1,0:T(8,128)(2,1)}, u32[]{:S(2)}) %copy-start.2) | copy-done | bytes 1376280
  4.2 0.0 copy-start.3
  4.2 0.8 %copy-done.3 = bf16[256,128]{1,0:T(8,128)(2,1)S(1)} copy-done((bf16[256,128]{1,0:T(8,128)(2,1)S(1)}, bf16[256,128]{1,0:T(8,128)(2,1)}, u32[]{:S(2)}) %copy-start.3) | copy-done | bytes 65560
  5.1 0.0 copy-start.4
  5.1 0.8 %copy-done.4 = bf16[256,128]{1,0:T(8,128)(2,1)S(1)} copy-done((bf16[256,128]{1,0:T(8,128)(2,1)S(1)}, bf16[256,128]{1,0:T(8,128)(2,1)}, u32[]{:S(2)}) %copy-start.4) | copy-done | bytes 65560
  5.9 0.0 copy-start.5
  5.9 0.8 %copy-done.5 = bf16[256,128]{1,0:T(8,128)(2,1)S(1)} copy-done((bf16[256,128]{1,0:T(8,128)(2,1)S(1)}, bf16[256,128]{1,0:T(8,128)(2,1)}, u32[]{:S(2)}) %copy-start.5) | copy-done | bytes 65560
  6.8 46.9 %shard_map.82 = bf16[256,1344]{1,0:T(8,128)(2,1)S(1)} custom-call(bf16[256,128]{1,0:T(8,128)(2,1)S(1)} %copy-done.3, bf16[256,128]{1,0:T(8,128)(2,1)S(1)} %copy-done.4, bf16[256,128]{1,0:T(8,128)(2,1)S(1)} %copy-done.5, bf16[256,1344]{1,0:T(8,128)(2,1)S(1)} %copy.9.d_out, bf16[128,5376]{1,0:T(8,128)(2,1)S(1)} %copy-done, bf16[5376,128]{1,0:T(8,128)(2,1)S(1)} %copy-done.1, ...), custom_call_target="tpu_custom_call" | custom-call | tf_op jit(solution)/shard_map/pallas_call | solution.py:442
  53.7 1.1 %copy.10 = bf16[256,1344]{0,1:T(8,128)(2,1)} copy(bf16[256,1344]{1,0:T(8,128)(2,1)S(1)} %shard_map.82) | data formatting | bytes 1376256 | tf_op jit(solution)/shard_map/pallas_call | solution.py:442
Async XLA Ops:
  0.0 1.6 %copy-start = (bf16[128,5376]{1,0:T(8,128)(2,1)S(1)}, bf16[128,5376]{1,0:T(8,128)(2,1)}, u32[]{:S(2)}) copy-start(bf16[128,5376]{1,0:T(8,128)(2,1)} %w_out.1) | copy-start | bytes 4128772
  1.6 1.3 %copy-start.1 = (bf16[5376,128]{1,0:T(8,128)(2,1)S(1)}, bf16[5376,128]{1,0:T(8,128)(2,1)}, u32[]{:S(2)}) copy-start(bf16[5376,128]{1,0:T(8,128)(2,1)} %w_query.1) | copy-start | bytes 4128772
  2.9 1.3 %copy-start.2 = (bf16[5376,128]{1,0:T(8,128)(2,1)S(1)}, bf16[5376,128]{1,0:T(8,128)(2,1)}, u32[]{:S(2)}) copy-start(bf16[5376,128]{1,0:T(8,128)(2,1)} %w_key.1) | copy-start | bytes 4128772
  4.2 0.8 %copy-start.3 = (bf16[256,128]{1,0:T(8,128)(2,1)S(1)}, bf16[256,128]{1,0:T(8,128)(2,1)}, u32[]{:S(2)}) copy-start(bf16[256,128]{1,0:T(8,128)(2,1)} %query.1) | copy-start | bytes 196612
  5.1 0.8 %copy-start.4 = (bf16[256,128]{1,0:T(8,128)(2,1)S(1)}, bf16[256,128]{1,0:T(8,128)(2,1)}, u32[]{:S(2)}) copy-start(bf16[256,128]{1,0:T(8,128)(2,1)} %keys.1) | copy-start | bytes 196612
  5.9 0.8 %copy-start.5 = (bf16[256,128]{1,0:T(8,128)(2,1)S(1)}, bf16[256,128]{1,0:T(8,128)(2,1)}, u32[]{:S(2)}) copy-start(bf16[256,128]{1,0:T(8,128)(2,1)} %values.1) | copy-start | bytes 196612

commit v2 on v1

--- a/solution.py
+++ b/solution.py
@@ -99,24 +99,22 @@
 ROW_CHUNKS = 4
 MESH = pl.DeviceIdType.MESH
 
-C_DOUT = 0
-C_WOUT = C_DOUT + ROW_CHUNKS
-C_HALO = C_WOUT + 2
+C_SIB = 0
+C_FAR = C_SIB + 3
+C_RELAY = C_FAR + 6
+C_HALO = C_RELAY + 9
 C_PASS = C_HALO + NBR
 C_PART = C_PASS + NBR
-C_WSIB = C_PART + 1
-C_WFAR = C_WSIB + 2
-C_WFWD = C_WFAR + 4
-C_SWAP = C_WFWD + 4
+C_SWAP = C_PART + 3
 C_BACK = C_SWAP + 1
 C_GRAD = C_BACK + NBR
 C_END = C_GRAD + 6
 
 
 def kernel(
-    seqs, query, keys, values, d_out, w_out, w_query, w_key, w_value, out,
-    wq_all, wkv_all, w_cut, w_own, w_sib, d_own, d_far, kv, probs, low, ds, partial, partial_in, heads,
-    parts, parts_in, back, back_in, grads, weights, total,
+    seqs, query_in, keys_in, values_in, d_out, w_out, w_query, w_key, w_value, out,
+    wq_all, wkv_all, wout_all, d_raw, d_own, w_cut, w_heads, query, kv, probs, low, ds,
+    own_part, partial, partial_in, parts, parts_in, back, back_in, grads, weights, total,
     send, recv, local,
 ):
     s = lax.axis_index("seq")
@@ -125,14 +123,29 @@
     sib = h + 1 - 2 * core
     across = lax.rem(h + 2, 4)
     diag = lax.rem(sib + 2, 4)
+    peers = (None, sib, across, diag)
     y = lax.rem(s, 2)
-    pair = s + 1 - 2 * y
-    peers = (None, sib, across, diag)
-    tokens = query.shape[0]
-    width = out.shape[1]
-    half = width // 2
+    z = lax.rem(s // 2, 2)
+    pair_y = s + 1 - 2 * y
+    pair_z = s + 2 - 4 * z
+    quarter = 2 * y + z
+    quarter_z = 2 * y + 1 - z
+    tokens, width = out.shape
+    wide = d_own.shape[1]
     reach = NBR
     f32, bf16 = jnp.float32, jnp.bfloat16
+
+    barrier = pltpu.get_barrier_semaphore()
+    for r in range(1, PEERS):
+        pl.semaphore_signal(barrier, inc=1, device_id=(s, peers[r]), device_id_type=MESH)
+    for d in range(1, reach + 1):
+        @pl.when(s >= d)
+        def _():
+            pl.semaphore_signal(barrier, inc=1, device_id=(s - d, h), device_id_type=MESH)
+
+        @pl.when(s + d < seqs)
+        def _():
+            pl.semaphore_signal(barrier, inc=1, device_id=(s + d, h), device_id_type=MESH)
 
     def remote(index, src, dst, seq, head):
         return pltpu.make_async_remote_copy(
@@ -140,10 +153,16 @@
             device_id=(seq, head), device_id_type=MESH,
         )
 
-    load_wq = pltpu.make_async_copy(w_query, wq_all, local.at[0])
-    load_wk = pltpu.make_async_copy(w_key, wkv_all, local.at[1])
-    load_wv = pltpu.make_async_copy(w_value, wkv_all, local.at[1])
-    load_wq.start()
+    load_wout = pltpu.make_async_copy(w_out, wout_all, local.at[0])
+    load_dout = pltpu.make_async_copy(d_out, d_raw, local.at[1])
+    load_keys = pltpu.make_async_copy(keys_in, kv.at[0, reach], local.at[2])
+    load_values = pltpu.make_async_copy(values_in, kv.at[1, reach], local.at[3])
+    load_query = pltpu.make_async_copy(query_in, query, local.at[4])
+    load_wq = pltpu.make_async_copy(w_query, wq_all, local.at[5])
+    load_wk = pltpu.make_async_copy(w_key, wkv_all, local.at[6])
+    load_wv = pltpu.make_async_copy(w_value, wkv_all, local.at[6])
+    for copy in (load_wout, load_keys, load_values, load_dout, load_query, load_wq):
+        copy.start()
 
     @pl.when(core == 0)
     def _():
@@ -153,39 +172,79 @@
     def _():
         load_wv.start()
 
-    wide = d_own.shape[1]
-    pad = jnp.zeros((HEAD, wide - width), bf16)
-    d_own[...] = jnp.concatenate([d_out[...], jnp.zeros((tokens, wide - width), bf16)], axis=1)
-    kv[0, reach] = keys[...]
-    kv[1, reach] = values[...]
     for d in range(1, reach + 1):
         @pl.when(s < d)
         def _():
             kv[0, reach - d] = jnp.zeros((tokens, HEAD), bf16)
             kv[1, reach - d] = jnp.zeros((tokens, HEAD), bf16)
 
-    barrier = pltpu.get_barrier_semaphore()
-    for r in range(1, PEERS):
-        pl.semaphore_signal(barrier, inc=1, device_id=(s, peers[r]), device_id_type=MESH)
-    for d in range(1, reach + 1):
-        @pl.when(s >= d)
-        def _():
-            pl.semaphore_signal(barrier, inc=1, device_id=(s - d, h), device_id_type=MESH)
-
-        @pl.when(s + d < seqs)
-        def _():
-            pl.semaphore_signal(barrier, inc=1, device_id=(s + d, h), device_id_type=MESH)
+    pad = jnp.zeros((HEAD, wide - width), bf16)
+    load_wout.wait()
+    for b in range(PEERS):
+        shift = b * width % 128
+        first = b * width - shift
+        room = min(width + 128, wout_all.shape[1] - first)
+        cut = wout_all[:, first : first + room][:, shift : shift + width]
+        cut = jnp.concatenate([cut, pad], axis=1)
+        w_cut[b] = cut
+
+        @pl.when(h == b)
+        def _():
+            w_heads[0] = cut
+
     behind = jnp.minimum(s, reach)
     ahead = jnp.minimum(seqs - 1 - s, reach)
     pl.semaphore_wait(barrier, PEERS - 1 + behind + ahead)
 
-    rows = tokens // ROW_CHUNKS
-    dout_copies = [
-        remote(C_DOUT + i, d_own.at[pl.ds(i * rows, rows)], d_far.at[pl.ds(i * rows, rows)], s, across)
-        for i in range(ROW_CHUNKS)
-    ]
-    for copy in dout_copies:
-        copy.start()
+    quarter_rows = (HEAD // 4, width // 4, width // 4)
+    slabs = (w_heads, weights.at[0], weights.at[1])
+    alls = (None, wq_all, wkv_all)
+
+    def rows_of(t, index):
+        size = quarter_rows[t]
+        return pl.ds(pl.multiple_of(index * size, 16), size)
+
+    def to_sib(t):
+        if t == 0:
+            src = w_cut.at[sib]
+        else:
+            src = alls[t].at[pl.ds(pl.multiple_of(sib * width, 16), width)]
+        return remote(C_SIB + t, src, slabs[t].at[SIB], s, sib)
+
+    def to_far(t, slot):
+        peer = peers[slot]
+        size = quarter_rows[t]
+        if t == 0:
+            src = w_cut.at[peer, rows_of(t, quarter)]
+        else:
+            src = alls[t].at[pl.ds(pl.multiple_of(peer * width + quarter * size, 16), size)]
+        dst = slabs[t].at[slot, rows_of(t, quarter)]
+        return remote(C_FAR + 2 * t + slot - ACROSS, src, dst, s, peer)
+
+    def relay(t, step):
+        index, target = ((quarter, pair_z), (quarter, pair_y), (quarter_z, pair_y))[step]
+        block = slabs[t].at[pl.ds(ACROSS, 2), rows_of(t, index)]
+        return remote(C_RELAY + 3 * t + step, block, block, target, h)
+
+    def relay_first(t):
+        for slot in (ACROSS, DIAG):
+            to_far(t, slot).wait_recv()
+        relay(t, 0).start()
+        relay(t, 1).start()
+
+    def relay_second(t):
+        relay(t, 0).wait_recv()
+        relay(t, 2).start()
+
+    def arrived(t):
+        relay(t, 1).wait_recv()
+        relay(t, 2).wait_recv()
+
+    for slot in (ACROSS, DIAG):
+        to_far(0, slot).start()
+    to_sib(0).start()
+    load_keys.wait()
+    load_values.wait()
     halo = [
         remote(C_HALO + d - 1, kv.at[core, reach], kv.at[core, reach - d], s + d, h)
         for d in range(1, reach + 1)
@@ -194,29 +253,34 @@
         @pl.when(s + d < seqs)
         def _():
             halo[d - 1].start()
-
-    for b in range(PEERS):
-        shift = b * width % 128
-        first = b * width - shift
-        room = min(width + 128, w_out.shape[1] - first)
-        cut = w_out[:, first : first + room][:, shift : shift + width]
-        cut = jnp.concatenate([cut, pad], axis=1)
-        w_cut[b] = cut
-
-        @pl.when(h == b)
-        def _():
-            w_own[0] = cut
-
-        @pl.when(across == b)
-        def _():
-            w_own[1] = cut
-    wout_copies = [
-        remote(C_WOUT, w_cut.at[sib], w_sib.at[0], s, sib),
-        remote(C_WOUT + 1, w_cut.at[diag], w_sib.at[1], s, sib),
+    load_dout.wait()
+    d_own[...] = jnp.concatenate([d_raw[...], jnp.zeros((tokens, wide - width), bf16)], axis=1)
+    relay_first(0)
+    load_wq.wait()
+    load_wk.wait()
+    load_own = []
+    for t in (1, 2):
+        rows_own = pl.ds(pl.multiple_of(h * width, 16), width)
+        load_own.append(
+            pltpu.make_async_copy(alls[t].at[rows_own], slabs[t].at[0], local.at[6 + t]))
+        for slot in (ACROSS, DIAG):
+            to_far(t, slot).start()
+
+    to_sib(0).wait_recv()
+    rows = tokens // ROW_CHUNKS
+    both_heads = 2 * HEAD
+    near = w_heads[0:2].reshape(both_heads, wide)
+    for i in range(ROW_CHUNKS):
+        here = pl.ds(i * rows, rows)
+        result = dot_rows(d_own[here, :], near)
+        own_part[here, :] = result[:, :HEAD]
+        partial[SIB - 1, here, :] = result[:, HEAD:].astype(bf16)
+    part = [
+        remote(C_PART + r - 1, partial.at[r - 1], partial_in.at[r - 1], s, peers[r])
+        for r in range(1, PEERS)
     ]
-    for copy in wout_copies:
-        copy.start()
-
+    part[SIB - 1].start()
+    relay_second(0)
     passed = [
         remote(C_PASS + d - 1, kv.at[core, reach - d], kv.at[core, reach - d], s, sib)
         for d in range(1, reach + 1)
@@ -226,23 +290,21 @@
         def _():
             halo[d - 1].wait_recv()
             passed[d - 1].start()
-
-    sib_rows = pl.ds(pl.multiple_of(sib * width, 16), width)
-    load_wq.wait()
-    load_wk.wait()
-    own_rows = pl.ds(pl.multiple_of(h * width, 16), width)
-    load_own = [
-        pltpu.make_async_copy(w.at[own_rows], weights.at[t, 0], local.at[2 + t])
-        for t, w in enumerate((wq_all, wkv_all))
-    ]
+    arrived(0)
+    far = w_heads[2:4].reshape(both_heads, wide)
+    for i in range(ROW_CHUNKS):
+        here = pl.ds(i * rows, rows)
+        result = dot_rows(d_own[here, :], far)
+        partial[ACROSS - 1, here, :] = result[:, :HEAD].astype(bf16)
+        partial[DIAG - 1, here, :] = result[:, HEAD:].astype(bf16)
+    part[ACROSS - 1].start()
+    part[DIAG - 1].start()
     for copy in load_own:
         copy.start()
-    wsib = [
-        remote(C_WSIB + t, w.at[sib_rows], weights.at[t, SIB], s, sib)
-        for t, w in enumerate((wq_all, wkv_all))
-    ]
-    for copy in wsib:
-        copy.start()
+    for t in (1, 2):
+        to_sib(t).start()
+    relay_first(1)
+    load_query.wait()
     for d in range(1, reach + 1):
         @pl.when(s >= d)
         def _():
@@ -276,47 +338,14 @@
             probs[here, j * tokens : (j + 1) * tokens] = p
             low[here, j * tokens : (j + 1) * tokens] = p.astype(bf16)
 
-    for copy in wout_copies:
+    relay_first(2)
+    relay_second(1)
+    for copy in part:
         copy.wait_recv()
-    for i in range(ROW_CHUNKS):
-        here = pl.ds(i * rows, rows)
-        heads[here, :] = dot_rows(d_own[here, :], w_own[0])
-        partial[here, :] = dot_rows(d_own[here, :], w_sib[0])
-    for i in range(ROW_CHUNKS):
-        here = pl.ds(i * rows, rows)
-        dout_copies[i].wait_recv()
-        partial[here, :] += dot_rows(d_far[here, :], w_sib[1])
-        heads[here, :] += dot_rows(d_far[here, :], w_own[1])
-    part = remote(C_PART, partial, partial_in, s, sib)
-    part.start()
-
-    wfar = []
-    for n, (slot, peer) in enumerate(((ACROSS, across), (DIAG, diag))):
-        src = pl.ds(pl.multiple_of(peer * width + y * half, 16), half)
-        dst = pl.ds(pl.multiple_of(y * half, 16), half)
-        wfar.append([
-            remote(C_WFAR + 2 * t + n, w.at[src], weights.at[t, slot, dst], s, peer)
-            for t, w in enumerate((wq_all, wkv_all))
-        ])
-    for copy in dout_copies:
-        copy.wait_send()
-    for t in range(2):
-        for far in wfar:
-            far[t].start()
-
-    def forward(t, n):
-        slot = (ACROSS, DIAG)[n]
-        mine = pl.ds(pl.multiple_of(y * half, 16), half)
-        block = weights.at[t, slot, mine]
-        return remote(C_WFWD + 2 * t + n, block, block, pair, h)
-
-    def relay(t):
-        for n in range(2):
-            wfar[n][t].wait_recv()
-            forward(t, n).start()
-
-    part.wait_recv()
-    grad_heads = (heads[...] + partial_in[...]).astype(bf16)
+    grad_heads = own_part[...]
+    for r in range(1, PEERS):
+        grad_heads = grad_heads + partial_in[r - 1].astype(f32)
+    grad_heads = grad_heads.astype(bf16)
 
     for j in range(reach + 1):
         parts[1, j] = dot_cols(low[:, j * tokens : (j + 1) * tokens], grad_heads).astype(bf16)
@@ -385,8 +414,7 @@
     share_query = share(0)
     for copy in share_query:
         copy.start()
-    relay(0)
-    relay(1)
+    relay_second(2)
     for d in range(1, reach + 1):
         @pl.when(s + d < seqs)
         def _():
@@ -397,13 +425,11 @@
     for copy in share_pair:
         copy.start()
 
-    for copy in wsib:
-        copy.wait_recv()
     for copy in load_own:
         copy.wait()
-    for t in range(2):
-        for n in range(2):
-            forward(t, n).wait_recv()
+    for t in (1, 2):
+        to_sib(t).wait_recv()
+        arrived(t)
     for copy in share_query + share_pair:
         copy.wait_recv()
     left = jnp.concatenate([grads[t, r] for t in range(2) for r in range(PEERS)], axis=1)
@@ -413,14 +439,14 @@
         acc = dot_rows(left, jnp.concatenate(right, axis=1))
         out[:, first : first + size] = acc.astype(bf16)
 
-    for copy in wout_copies + share_query + share_pair:
+    for copy in part + share_query + share_pair + [swap]:
         copy.wait_send()
-    for copy in (part, wsib[0], wsib[1], swap):
-        copy.wait_send()
-    for t in range(2):
-        for n in range(2):
-            wfar[n][t].wait_send()
-            forward(t, n).wait_send()
+    for t in range(3):
+        to_sib(t).wait_send()
+        for slot in (ACROSS, DIAG):
+            to_far(t, slot).wait_send()
+        for step in range(3):
+            relay(t, step).wait_send()
     for d in range(1, reach + 1):
         @pl.when(s + d < seqs)
         def _():
@@ -438,27 +464,28 @@
     span = (NBR + 1) * tokens
     bf16, f32 = jnp.bfloat16, jnp.float32
     vmem = pl.BlockSpec(memory_space=pltpu.VMEM)
-    anywhere = pl.BlockSpec(memory_space=pl.ANY)
+    hbm = pl.BlockSpec(memory_space=pltpu.HBM)
     return pl.pallas_call(
         functools.partial(kernel, seqs),
         out_shape=jax.ShapeDtypeStruct((tokens, width), bf16),
-        in_specs=[vmem] * 5 + [anywhere] * 3,
+        in_specs=[hbm] * 8,
         out_specs=vmem,
         scratch_shapes=[
             pltpu.VMEM(w_query.shape, bf16),
             pltpu.VMEM(w_key.shape, bf16),
+            pltpu.VMEM(w_out.shape, bf16),
+            pltpu.VMEM((tokens, width), bf16),
+            pltpu.VMEM((tokens, wide), bf16),
             pltpu.VMEM((PEERS, HEAD, wide), bf16),
-            pltpu.VMEM((2, HEAD, wide), bf16),
-            pltpu.VMEM((2, HEAD, wide), bf16),
-            pltpu.VMEM((tokens, wide), bf16),
-            pltpu.VMEM((tokens, wide), bf16),
+            pltpu.VMEM((PEERS, HEAD, wide), bf16),
+            pltpu.VMEM((tokens, HEAD), bf16),
             pltpu.VMEM((2, NBR + 1, tokens, HEAD), bf16),
             pltpu.VMEM((tokens, span), f32),
             pltpu.VMEM((tokens, span), bf16),
             pltpu.VMEM((tokens, span), bf16),
             pltpu.VMEM((tokens, HEAD), f32),
-            pltpu.VMEM((tokens, HEAD), f32),
-            pltpu.VMEM((tokens, HEAD), f32),
+            pltpu.VMEM((PEERS - 1, tokens, HEAD), bf16),
+            pltpu.VMEM((PEERS - 1, tokens, HEAD), bf16),
             pltpu.VMEM((2, NBR + 1, tokens, HEAD), bf16),
             pltpu.VMEM((NBR + 1, tokens, HEAD), bf16),
             pltpu.VMEM((NBR, tokens, HEAD), bf16),
@@ -468,7 +495,7 @@
             pltpu.VMEM((tokens, HEAD), f32),
             pltpu.SemaphoreType.DMA((C_END,)),
             pltpu.SemaphoreType.DMA((C_END,)),
-            pltpu.SemaphoreType.DMA((4,)),
+            pltpu.SemaphoreType.DMA((9,)),
         ],
         compiler_params=pltpu.CompilerParams(
             collective_id=0, has_side_effects=True, vmem_limit_bytes=48 * 1024 * 1024,
@@ -493,8 +520,8 @@
     def local(query, keys, values, d_out, w_out, w_query, w_key, w_value):
         args = (query, keys, values, d_out, w_out, w_query, w_key, w_value)
         tokens, width = d_out.shape
-        fits = peers == PEERS and seqs % 2 == 0 and query.shape[1] == HEAD
-        fits = fits and tokens * NBR == WINDOW and width % 32 == 0
+        fits = peers == PEERS and seqs % 4 == 0 and query.shape[1] == HEAD
+        fits = fits and tokens * NBR == WINDOW and width % 64 == 0
         return fused(seqs, *args) if fits else body(*args)
 
     return jax.shard_map(local, mesh=mesh, in_specs=in_specs, out_specs=out_specs, check_vma=False)

time: 55.2 us -> 56.1 us (1.016)
  the two profiles are of different devices: /device:TPU:0 before, /device:TPU:13 now
where the time goes in v2:
time: 56.1 us; the launch traced here: 55.8 us
  Pallas kernels  47.9 us (85%)
  local copies, waits for them, and re-layouts  7.85 us (14%)
    pallas_call x1, Pallas kernels, fused(): pl.pallas_call(functools.partial(kernel, seqs), out_shape=jax.ShapeDtypeS...  47.9 us
    unnamed x13, local copies, waits for them, and re-layouts  6.74 us

profile of v2, /device:TPU:13, one launch (start us, length us, event | category | flops | bytes accessed | tf_op | source)
XLA Modules:
  0.0 55.8 jit_solution(16732684619601076711)
XLA Ops:
  0.0 0.0 copy-start
  0.0 1.5 %copy.9.d_out = bf16[256,1344]{1,0:T(8,128)(2,1)S(1)} copy(bf16[256,1344]{0,1:T(8,128)(2,1)} %param.11) | data formatting | bytes 1376256 | tf_op args[3]
  1.5 0.0 copy-done
  1.6 0.0 copy-start.1
  1.6 1.3 %copy-done.1 = bf16[5376,128]{1,0:T(8,128)(2,1)S(1)} copy-done((bf16[5376,128]{1,0:T(8,128)(2,1)S(1)}, bf16[5376,128]{1,0:T(8,128)(2,1)}, u32[]{:S(2)}) %copy-start.1) | copy-done | bytes 1376280
  2.9 0.0 copy-start.2
  2.9 1.3 %copy-done.2 = bf16[5376,128]{1,0:T(8,128)(2,1)S(1)} copy-done((bf16[5376,128]{1,0:T(8,128)(2,1)S(1)}, bf16[5376,128]{1,0:T(8,128)(2,1)}, u32[]{:S(2)}) %copy-start.2) | copy-done | bytes 1376280
  4.2 0.0 copy-start.3
  4.2 0.8 %copy-done.3 = bf16[256,128]{1,0:T(8,128)(2,1)S(1)} copy-done((bf16[256,128]{1,0:T(8,128)(2,1)S(1)}, bf16[256,128]{1,0:T(8,128)(2,1)}, u32[]{:S(2)}) %copy-start.3) | copy-done | bytes 65560
  5.1 0.0 copy-start.4
  5.1 0.8 %copy-done.4 = bf16[256,128]{1,0:T(8,128)(2,1)S(1)} copy-done((bf16[256,128]{1,0:T(8,128)(2,1)S(1)}, bf16[256,128]{1,0:T(8,128)(2,1)}, u32[]{:S(2)}) %copy-start.4) | copy-done | bytes 65560
  5.9 0.0 copy-start.5
  5.9 0.8 %copy-done.5 = bf16[256,128]{1,0:T(8,128)(2,1)S(1)} copy-done((bf16[256,128]{1,0:T(8,128)(2,1)S(1)}, bf16[256,128]{1,0:T(8,128)(2,1)}, u32[]{:S(2)}) %copy-start.5) | copy-done | bytes 65560
  6.8 47.9 %shard_map.82 = bf16[256,1344]{1,0:T(8,128)(2,1)S(1)} custom-call(bf16[256,128]{1,0:T(8,128)(2,1)S(1)} %copy-done.3, bf16[256,128]{1,0:T(8,128)(2,1)S(1)} %copy-done.4, bf16[256,128]{1,0:T(8,128)(2,1)S(1)} %copy-done.5, bf16[256,1344]{1,0:T(8,128)(2,1)S(1)} %copy.9.d_out, bf16[128,5376]{1,0:T(8,128)(2,1)S(1)} %copy-done, bf16[5376,128]{1,0:T(8,128)(2,1)S(1)} %copy-done.1, ...), custom_call_target="tpu_custom_call" | custom-call | tf_op jit(solution)/shard_map/pallas_call | solution.py:468
  54.7 1.1 %copy.10 = bf16[256,1344]{0,1:T(8,128)(2,1)} copy(bf16[256,1344]{1,0:T(8,128)(2,1)S(1)} %shard_map.82) | data formatting | bytes 1376256 | tf_op jit(solution)/shard_map/pallas_call | solution.py:468
Async XLA Ops:
  0.0 1.6 %copy-start = (bf16[128,5376]{1,0:T(8,128)(2,1)S(1)}, bf16[128,5376]{1,0:T(8,128)(2,1)}, u32[]{:S(2)}) copy-start(bf16[128,5376]{1,0:T(8,128)(2,1)} %w_out.1) | copy-start | bytes 4128772
  1.6 1.3 %copy-start.1 = (bf16[5376,128]{1,0:T(8,128)(2,1)S(1)}, bf16[5376,128]{1,0:T(8,128)(2,1)}, u32[]{:S(2)}) copy-start(bf16[5376,128]{1,0:T(8,128)(2,1)} %w_query.1) | copy-start | bytes 4128772
  2.9 1.3 %copy-start.2 = (bf16[5376,128]{1,0:T(8,128)(2,1)S(1)}, bf16[5376,128]{1,0:T(8,128)(2,1)}, u32[]{:S(2)}) copy-start(bf16[5376,128]{1,0:T(8,128)(2,1)} %w_key.1) | copy-start | bytes 4128772
  4.2 0.8 %copy-start.3 = (bf16[256,128]{1,0:T(8,128)(2,1)S(1)}, bf16[256,128]{1,0:T(8,128)(2,1)}, u32[]{:S(2)}) copy-start(bf16[256,128]{1,0:T(8,128)(2,1)} %query_in.1) | copy-start | bytes 196612
  5.1 0.8 %copy-start.4 = (bf16[256,128]{1,0:T(8,128)(2,1)S(1)}, bf16[256,128]{1,0:T(8,128)(2,1)}, u32[]{:S(2)}) copy-start(bf16[256,128]{1,0:T(8,128)(2,1)} %keys_in.1) | copy-start | bytes 196612
  5.9 0.8 %copy-start.5 = (bf16[256,128]{1,0:T(8,128)(2,1)S(1)}, bf16[256,128]{1,0:T(8,128)(2,1)}, u32[]{:S(2)}) copy-start(bf16[256,128]{1,0:T(8,128)(2,1)} %values_in.1) | copy-start | bytes 196612

commit v3 on v2

--- a/solution.py
+++ b/solution.py
@@ -101,8 +101,8 @@
 
 C_SIB = 0
 C_FAR = C_SIB + 3
-C_RELAY = C_FAR + 6
-C_HALO = C_RELAY + 9
+C_RELAY = C_FAR + 8
+C_HALO = C_RELAY + 24
 C_PASS = C_HALO + NBR
 C_PART = C_PASS + NBR
 C_SWAP = C_PART + 3
@@ -113,8 +113,8 @@
 
 def kernel(
     seqs, query_in, keys_in, values_in, d_out, w_out, w_query, w_key, w_value, out,
-    wq_all, wkv_all, wout_all, d_raw, d_own, w_cut, w_heads, query, kv, probs, low, ds,
-    own_part, partial, partial_in, parts, parts_in, back, back_in, grads, weights, total,
+    wq_all, wkv_all, wout_all, d_own, w_cut, w_heads, query, kv, probs, low, ds,
+    own_part, partial, partial_in, parts, parts_in, back, back_in, grads, weights, total, acc,
     send, recv, local,
 ):
     s = lax.axis_index("seq")
@@ -130,8 +130,9 @@
     pair_z = s + 2 - 4 * z
     quarter = 2 * y + z
     quarter_z = 2 * y + 1 - z
-    tokens, width = out.shape
-    wide = d_own.shape[1]
+    quarter_y = 2 - 2 * y + z
+    width, tokens = out.shape
+    wide = d_own.shape[0]
     reach = NBR
     f32, bf16 = jnp.float32, jnp.bfloat16
 
@@ -154,7 +155,7 @@
         )
 
     load_wout = pltpu.make_async_copy(w_out, wout_all, local.at[0])
-    load_dout = pltpu.make_async_copy(d_out, d_raw, local.at[1])
+    load_dout = pltpu.make_async_copy(d_out, d_own.at[pl.ds(0, width)], local.at[1])
     load_keys = pltpu.make_async_copy(keys_in, kv.at[0, reach], local.at[2])
     load_values = pltpu.make_async_copy(values_in, kv.at[1, reach], local.at[3])
     load_query = pltpu.make_async_copy(query_in, query, local.at[4])
@@ -177,6 +178,8 @@
         def _():
             kv[0, reach - d] = jnp.zeros((tokens, HEAD), bf16)
             kv[1, reach - d] = jnp.zeros((tokens, HEAD), bf16)
+
+    d_own[width:wide] = jnp.zeros((wide - width, tokens), bf16)
 
     pad = jnp.zeros((HEAD, wide - width), bf16)
     load_wout.wait()
@@ -196,13 +199,16 @@
     ahead = jnp.minimum(seqs - 1 - s, reach)
     pl.semaphore_wait(barrier, PEERS - 1 + behind + ahead)
 
-    quarter_rows = (HEAD // 4, width // 4, width // 4)
+    piece = (HEAD // 8, HEAD // 8, width // 4, width // 4)
+    slab_of = (0, 0, 1, 2)
     slabs = (w_heads, weights.at[0], weights.at[1])
     alls = (None, wq_all, wkv_all)
 
-    def rows_of(t, index):
-        size = quarter_rows[t]
-        return pl.ds(pl.multiple_of(index * size, 16), size)
+    def start_of(i, index):
+        return index * 2 * piece[i] + i * piece[i] if i < 2 else index * piece[i]
+
+    def rows_of(i, index):
+        return pl.ds(pl.multiple_of(start_of(i, index), 16), piece[i])
 
     def to_sib(t):
         if t == 0:
@@ -211,37 +217,49 @@
             src = alls[t].at[pl.ds(pl.multiple_of(sib * width, 16), width)]
         return remote(C_SIB + t, src, slabs[t].at[SIB], s, sib)
 
-    def to_far(t, slot):
+    def to_far(i, slot):
         peer = peers[slot]
-        size = quarter_rows[t]
+        t = slab_of[i]
         if t == 0:
-            src = w_cut.at[peer, rows_of(t, quarter)]
+            src = w_cut.at[peer, rows_of(i, quarter)]
         else:
-            src = alls[t].at[pl.ds(pl.multiple_of(peer * width + quarter * size, 16), size)]
-        dst = slabs[t].at[slot, rows_of(t, quarter)]
-        return remote(C_FAR + 2 * t + slot - ACROSS, src, dst, s, peer)
-
-    def relay(t, step):
-        index, target = ((quarter, pair_z), (quarter, pair_y), (quarter_z, pair_y))[step]
-        block = slabs[t].at[pl.ds(ACROSS, 2), rows_of(t, index)]
-        return remote(C_RELAY + 3 * t + step, block, block, target, h)
-
-    def relay_first(t):
+            first = peer * width + start_of(i, quarter)
+            src = alls[t].at[pl.ds(pl.multiple_of(first, 16), piece[i])]
+        dst = slabs[t].at[slot, rows_of(i, quarter)]
+        return remote(C_FAR + 2 * i + slot - ACROSS, src, dst, s, peer)
+
+    def relay(i, slot, step):
+        if step < 2:
+            index, target = quarter, (pair_z, pair_y)[step]
+        elif slab_of[i] == 0 and slot == DIAG:
+            index, target = quarter_y, pair_z
+        else:
+            index, target = quarter_z, pair_y
+        block = slabs[slab_of[i]].at[slot, rows_of(i, index)]
+        number = 6 * i + 3 * (slot - ACROSS) + step
+        return remote(C_RELAY + number, block, block, target, h)
+
+    def relay_first(i):
         for slot in (ACROSS, DIAG):
-            to_far(t, slot).wait_recv()
-        relay(t, 0).start()
-        relay(t, 1).start()
-
-    def relay_second(t):
-        relay(t, 0).wait_recv()
-        relay(t, 2).start()
-
-    def arrived(t):
-        relay(t, 1).wait_recv()
-        relay(t, 2).wait_recv()
-
-    for slot in (ACROSS, DIAG):
-        to_far(0, slot).start()
+            to_far(i, slot).wait_recv()
+            relay(i, slot, 0).start()
+            relay(i, slot, 1).start()
+
+    def relay_second(i):
+        for slot in (ACROSS, DIAG):
+            over_y = slab_of[i] == 0 and slot == DIAG
+            relay(i, slot, 1 if over_y else 0).wait_recv()
+            relay(i, slot, 2).start()
+
+    def arrived(i):
+        for slot in (ACROSS, DIAG):
+            over_y = slab_of[i] == 0 and slot == DIAG
+            relay(i, slot, 0 if over_y else 1).wait_recv()
+            relay(i, slot, 2).wait_recv()
+
+    for i in (0, 1):
+        for slot in (ACROSS, DIAG):
+            to_far(i, slot).start()
     to_sib(0).start()
     load_keys.wait()
     load_values.wait()
@@ -249,13 +267,32 @@
         remote(C_HALO + d - 1, kv.at[core, reach], kv.at[core, reach - d], s + d, h)
         for d in range(1, reach + 1)
     ]
-    for d in range(1, reach + 1):
-        @pl.when(s + d < seqs)
-        def _():
-            halo[d - 1].start()
+    passed = [
+        remote(C_PASS + d - 1, kv.at[core, reach - d], kv.at[core, reach - d], s, sib)
+        for d in range(1, reach + 1)
+    ]
+
+    def send_halo(which):
+        for d in range(1, reach + 1):
+            @pl.when((core == which) & (s + d < seqs))
+            def _():
+                halo[d - 1].start()
+
+    def pass_halo(which):
+        for d in range(1, reach + 1):
+            @pl.when((core == which) & (s >= d))
+            def _():
+                halo[d - 1].wait_recv()
+                passed[d - 1].start()
+
+    def get_halo(which):
+        for d in range(1, reach + 1):
+            @pl.when((core != which) & (s >= d))
+            def _():
+                passed[d - 1].wait_recv()
+
+    send_halo(0)
     load_dout.wait()
-    d_own[...] = jnp.concatenate([d_raw[...], jnp.zeros((tokens, wide - width), bf16)], axis=1)
-    relay_first(0)
     load_wq.wait()
     load_wk.wait()
     load_own = []
@@ -263,52 +300,43 @@
         rows_own = pl.ds(pl.multiple_of(h * width, 16), width)
         load_own.append(
             pltpu.make_async_copy(alls[t].at[rows_own], slabs[t].at[0], local.at[6 + t]))
-        for slot in (ACROSS, DIAG):
-            to_far(t, slot).start()
+    relay_first(0)
+    relay_first(1)
+    for slot in (ACROSS, DIAG):
+        to_far(2, slot).start()
 
     to_sib(0).wait_recv()
     rows = tokens // ROW_CHUNKS
     both_heads = 2 * HEAD
+    d_all = d_own[...]
     near = w_heads[0:2].reshape(both_heads, wide)
-    for i in range(ROW_CHUNKS):
-        here = pl.ds(i * rows, rows)
-        result = dot_rows(d_own[here, :], near)
-        own_part[here, :] = result[:, :HEAD]
-        partial[SIB - 1, here, :] = result[:, HEAD:].astype(bf16)
+    result = jnp.dot(near, d_all, preferred_element_type=f32).T
+    own_part[...] = result[:, :HEAD]
+    partial[SIB - 1] = result[:, HEAD:].astype(bf16)
     part = [
         remote(C_PART + r - 1, partial.at[r - 1], partial_in.at[r - 1], s, peers[r])
         for r in range(1, PEERS)
     ]
     part[SIB - 1].start()
     relay_second(0)
-    passed = [
-        remote(C_PASS + d - 1, kv.at[core, reach - d], kv.at[core, reach - d], s, sib)
-        for d in range(1, reach + 1)
-    ]
-    for d in range(1, reach + 1):
-        @pl.when(s >= d)
-        def _():
-            halo[d - 1].wait_recv()
-            passed[d - 1].start()
+    relay_second(1)
+    send_halo(1)
+    pass_halo(0)
     arrived(0)
+    arrived(1)
     far = w_heads[2:4].reshape(both_heads, wide)
-    for i in range(ROW_CHUNKS):
-        here = pl.ds(i * rows, rows)
-        result = dot_rows(d_own[here, :], far)
-        partial[ACROSS - 1, here, :] = result[:, :HEAD].astype(bf16)
-        partial[DIAG - 1, here, :] = result[:, HEAD:].astype(bf16)
+    result = jnp.dot(far, d_all, preferred_element_type=f32).T.astype(bf16)
+    partial[ACROSS - 1] = result[:, :HEAD]
+    partial[DIAG - 1] = result[:, HEAD:]
     part[ACROSS - 1].start()
     part[DIAG - 1].start()
     for copy in load_own:
         copy.start()
     for t in (1, 2):
         to_sib(t).start()
-    relay_first(1)
+    relay_first(2)
     load_query.wait()
-    for d in range(1, reach + 1):
-        @pl.when(s >= d)
-        def _():
-            passed[d - 1].wait_recv()
+    get_halo(0)
 
     for i in range(ROW_CHUNKS):
         here = pl.ds(i * rows, rows)
@@ -338,10 +366,12 @@
             probs[here, j * tokens : (j + 1) * tokens] = p
             low[here, j * tokens : (j + 1) * tokens] = p.astype(bf16)
 
-    relay_first(2)
-    relay_second(1)
+    pass_halo(1)
+    relay_second(2)
     for copy in part:
         copy.wait_recv()
+    for slot in (ACROSS, DIAG):
+        to_far(3, slot).start()
     grad_heads = own_part[...]
     for r in range(1, PEERS):
         grad_heads = grad_heads + partial_in[r - 1].astype(f32)
@@ -355,7 +385,31 @@
     def _():
         swap.start()
 
+    back_copies = [
+        remote(C_BACK + d - 1, back.at[reach - d], back_in.at[d - 1], s - d, h)
+        for d in range(1, reach + 1)
+    ]
+
+    def send_back(which):
+        @pl.when(core == which)
+        def _():
+            swap.wait_recv()
+            for d in range(reach, -1, -1):
+                j = reach - d
+                both = parts[which, j].astype(f32) + parts_in[j].astype(f32)
+                if d == 0:
+                    total[...] = both
+                else:
+                    back[j] = both.astype(bf16)
+
+                    @pl.when(s >= d)
+                    def _():
+                        back_copies[d - 1].start()
+
+    get_halo(1)
     for i in range(ROW_CHUNKS):
+        if i == ROW_CHUNKS // 2:
+            send_back(1)
         here = pl.ds(i * rows, rows)
         block = grad_heads[i * rows : (i + 1) * rows]
         weighted = []
@@ -387,23 +441,7 @@
             ds[:, j * tokens : (j + 1) * tokens], kv[0, j], preferred_element_type=f32)
     grads[0, 0] = (grad_query * score_scale).astype(bf16)
 
-    swap.wait_recv()
-    back_copies = [
-        remote(C_BACK + d - 1, back.at[reach - d], back_in.at[d - 1], s - d, h)
-        for d in range(1, reach + 1)
-    ]
-    for d in range(reach, -1, -1):
-        j = reach - d
-        kept = jnp.where(core == 0, parts[0, j].astype(f32), parts[1, j].astype(f32))
-        both = kept + parts_in[j].astype(f32)
-        if d == 0:
-            total[...] = both
-        else:
-            back[j] = both.astype(bf16)
-
-            @pl.when(s >= d)
-            def _():
-                back_copies[d - 1].start()
+    send_back(0)
 
     def share(t):
         return [
@@ -414,7 +452,24 @@
     share_query = share(0)
     for copy in share_query:
         copy.start()
-    relay_second(2)
+    relay_first(3)
+
+    for copy in share_query:
+        copy.wait_recv()
+    load_own[0].wait()
+    to_sib(1).wait_recv()
+    arrived(2)
+    chunk = width // 7
+
+    def product(t, first):
+        right = jnp.concatenate([grads[t, r] for r in range(PEERS)], axis=1)
+        left = jnp.concatenate(
+            [weights[t, r, first : first + chunk] for r in range(PEERS)], axis=1)
+        return dot_rows(left, right)
+
+    for first in range(0, width, chunk):
+        acc[first : first + chunk] = product(0, first)
+    relay_second(3)
     for d in range(1, reach + 1):
         @pl.when(s + d < seqs)
         def _():
@@ -425,28 +480,24 @@
     for copy in share_pair:
         copy.start()
 
-    for copy in load_own:
-        copy.wait()
-    for t in (1, 2):
-        to_sib(t).wait_recv()
-        arrived(t)
-    for copy in share_query + share_pair:
+    load_own[1].wait()
+    to_sib(2).wait_recv()
+    arrived(3)
+    for copy in share_pair:
         copy.wait_recv()
-    left = jnp.concatenate([grads[t, r] for t in range(2) for r in range(PEERS)], axis=1)
-    for first in range(0, width, 256):
-        size = min(256, width - first)
-        right = [weights[t, r, first : first + size] for t in range(2) for r in range(PEERS)]
-        acc = dot_rows(left, jnp.concatenate(right, axis=1))
-        out[:, first : first + size] = acc.astype(bf16)
+    for first in range(0, width, chunk):
+        here = slice(first, first + chunk)
+        out[here] = (acc[here] + product(1, first)).astype(bf16)
 
     for copy in part + share_query + share_pair + [swap]:
         copy.wait_send()
     for t in range(3):
         to_sib(t).wait_send()
+    for i in range(4):
         for slot in (ACROSS, DIAG):
-            to_far(t, slot).wait_send()
-        for step in range(3):
-            relay(t, step).wait_send()
+            to_far(i, slot).wait_send()
+            for step in range(3):
+                relay(i, slot, step).wait_send()
     for d in range(1, reach + 1):
         @pl.when(s + d < seqs)
         def _():
@@ -467,15 +518,14 @@
     hbm = pl.BlockSpec(memory_space=pltpu.HBM)
     return pl.pallas_call(
         functools.partial(kernel, seqs),
-        out_shape=jax.ShapeDtypeStruct((tokens, width), bf16),
+        out_shape=jax.ShapeDtypeStruct((width, tokens), bf16),
         in_specs=[hbm] * 8,
         out_specs=vmem,
         scratch_shapes=[
             pltpu.VMEM(w_query.shape, bf16),
             pltpu.VMEM(w_key.shape, bf16),
             pltpu.VMEM(w_out.shape, bf16),
-            pltpu.VMEM((tokens, width), bf16),
-            pltpu.VMEM((tokens, wide), bf16),
+            pltpu.VMEM((wide, tokens), bf16),
             pltpu.VMEM((PEERS, HEAD, wide), bf16),
             pltpu.VMEM((PEERS, HEAD, wide), bf16),
             pltpu.VMEM((tokens, HEAD), bf16),
@@ -493,14 +543,15 @@
             pltpu.VMEM((2, PEERS, tokens, HEAD), bf16),
             pltpu.VMEM((2, PEERS, width, HEAD), bf16),
             pltpu.VMEM((tokens, HEAD), f32),
+            pltpu.VMEM((width, tokens), f32),
             pltpu.SemaphoreType.DMA((C_END,)),
             pltpu.SemaphoreType.DMA((C_END,)),
             pltpu.SemaphoreType.DMA((9,)),
         ],
         compiler_params=pltpu.CompilerParams(
-            collective_id=0, has_side_effects=True, vmem_limit_bytes=48 * 1024 * 1024,
+            collective_id=0, has_side_effects=True, vmem_limit_bytes=63 * 1024 * 1024,
         ),
-    )(query, keys, values, d_out, w_out, w_query, w_key, w_value)
+    )(query, keys, values, d_out.T, w_out, w_query, w_key, w_value).T
 
 
 def solution(mesh):
@@ -521,7 +572,7 @@
         args = (query, keys, values, d_out, w_out, w_query, w_key, w_value)
         tokens, width = d_out.shape
         fits = peers == PEERS and seqs % 4 == 0 and query.shape[1] == HEAD
-        fits = fits and tokens * NBR == WINDOW and width % 64 == 0
+        fits = fits and tokens * NBR == WINDOW and width % (64 * 7) == 0
         return fused(seqs, *args) if fits else body(*args)
 
     return jax.shard_map(local, mesh=mesh, in_specs=in_specs, out_specs=out_specs, check_vma=False)

time: 56.1 us -> 45.2 us (0.81)
  the two profiles are of different devices: /device:TPU:13 before, /device:TPU:0 now
where the time goes in v3:
time: 45.2 us; the launch traced here: 45 us
  Pallas kernels  43 us (95%)
  local copies, waits for them, and re-layouts  1.99 us (4%)
    pallas_call x1, Pallas kernels, fused(): pl.pallas_call(functools.partial(kernel, seqs), out_shape=jax.ShapeDtypeS...  43 us
    unnamed x1, local copies, waits for them, and re-layouts  1.99 us

profile of v3, /device:TPU:0, one launch (start us, length us, event | category | flops | bytes accessed | tf_op | source)
XLA Modules:
  0.0 45.0 jit_solution(13307656088519819447)
XLA Ops:
  0.0 43.0 %shard_map.82 = bf16[1344,256]{1,0:T(8,128)(2,1)} custom-call(bf16[256,128]{1,0:T(8,128)(2,1)} %query_in.1, bf16[256,128]{1,0:T(8,128)(2,1)} %keys_in.1, bf16[256,128]{1,0:T(8,128)(2,1)} %values_in.1, bf16[1344,256]{1,0:T(8,128)(2,1)} %bitcast.3, bf16[128,5376]{1,0:T(8,128)(2,1)} %w_out.1, bf16[5376,128]{1,0:T(8,128)(2,1)} %w_query.1, ...), custom_call_target="tpu_custom_call" | custom-call | tf_op jit(solution)/shard_map/pallas_call | solution.py:519
  43.0 2.0 %copy.10 = bf16[256,1344]{0,1:T(8,128)(2,1)} copy(bf16[256,1344]{0,1:T(8,128)(2,1)} %bitcast.2) | data formatting | bytes 1376256

commit v4 on v3

--- a/solution.py
+++ b/solution.py
@@ -101,8 +101,8 @@
 
 C_SIB = 0
 C_FAR = C_SIB + 3
-C_RELAY = C_FAR + 8
-C_HALO = C_RELAY + 24
+C_RELAY = C_FAR + 10
+C_HALO = C_RELAY + 30
 C_PASS = C_HALO + NBR
 C_PART = C_PASS + NBR
 C_SWAP = C_PART + 3
@@ -162,8 +162,20 @@
     load_wq = pltpu.make_async_copy(w_query, wq_all, local.at[5])
     load_wk = pltpu.make_async_copy(w_key, wkv_all, local.at[6])
     load_wv = pltpu.make_async_copy(w_value, wkv_all, local.at[6])
-    for copy in (load_wout, load_keys, load_values, load_dout, load_query, load_wq):
+    for copy in (load_wout, load_keys, load_values, load_dout, load_query):
         copy.start()
+
+    for d in range(1, reach + 1):
+        @pl.when(s < d)
+        def _():
+            kv[0, reach - d] = jnp.zeros((tokens, HEAD), bf16)
+            kv[1, reach - d] = jnp.zeros((tokens, HEAD), bf16)
+
+    d_own[width:wide] = jnp.zeros((wide - width, tokens), bf16)
+
+    pad = jnp.zeros((HEAD, wide - width), bf16)
+    load_wout.wait()
+    load_wq.start()
 
     @pl.when(core == 0)
     def _():
@@ -173,16 +185,6 @@
     def _():
         load_wv.start()
 
-    for d in range(1, reach + 1):
-        @pl.when(s < d)
-        def _():
-            kv[0, reach - d] = jnp.zeros((tokens, HEAD), bf16)
-            kv[1, reach - d] = jnp.zeros((tokens, HEAD), bf16)
-
-    d_own[width:wide] = jnp.zeros((wide - width, tokens), bf16)
-
-    pad = jnp.zeros((HEAD, wide - width), bf16)
-    load_wout.wait()
     for b in range(PEERS):
         shift = b * width % 128
         first = b * width - shift
@@ -199,13 +201,17 @@
     ahead = jnp.minimum(seqs - 1 - s, reach)
     pl.semaphore_wait(barrier, PEERS - 1 + behind + ahead)
 
-    piece = (HEAD // 8, HEAD // 8, width // 4, width // 4)
-    slab_of = (0, 0, 1, 2)
+    piece = (HEAD // 8, HEAD // 8, width // 4, width // 4, width // 4)
+    slab_of = (0, 0, 1, 2, 2)
     slabs = (w_heads, weights.at[0], weights.at[1])
     alls = (None, wq_all, wkv_all)
 
     def start_of(i, index):
-        return index * 2 * piece[i] + i * piece[i] if i < 2 else index * piece[i]
+        if slab_of[i] == 0:
+            return (index * 2 + i) * piece[i]
+        if slab_of[i] == 1:
+            return index * piece[i]
+        return (2 * y + i - 3) * piece[i]
 
     def rows_of(i, index):
         return pl.ds(pl.multiple_of(start_of(i, index), 16), piece[i])
@@ -239,11 +245,14 @@
         number = 6 * i + 3 * (slot - ACROSS) + step
         return remote(C_RELAY + number, block, block, target, h)
 
+    def steps_of(i):
+        return (1,) if slab_of[i] == 2 else (0, 1, 2)
+
     def relay_first(i):
         for slot in (ACROSS, DIAG):
             to_far(i, slot).wait_recv()
-            relay(i, slot, 0).start()
-            relay(i, slot, 1).start()
+            for step in steps_of(i)[:2]:
+                relay(i, slot, step).start()
 
     def relay_second(i):
         for slot in (ACROSS, DIAG):
@@ -255,7 +264,8 @@
         for slot in (ACROSS, DIAG):
             over_y = slab_of[i] == 0 and slot == DIAG
             relay(i, slot, 0 if over_y else 1).wait_recv()
-            relay(i, slot, 2).wait_recv()
+            if slab_of[i] < 2:
+                relay(i, slot, 2).wait_recv()
 
     for i in (0, 1):
         for slot in (ACROSS, DIAG):
@@ -370,8 +380,9 @@
     relay_second(2)
     for copy in part:
         copy.wait_recv()
-    for slot in (ACROSS, DIAG):
-        to_far(3, slot).start()
+    for i in (3, 4):
+        for slot in (ACROSS, DIAG):
+            to_far(i, slot).start()
     grad_heads = own_part[...]
     for r in range(1, PEERS):
         grad_heads = grad_heads + partial_in[r - 1].astype(f32)
@@ -469,7 +480,7 @@
 
     for first in range(0, width, chunk):
         acc[first : first + chunk] = product(0, first)
-    relay_second(3)
+    relay_first(4)
     for d in range(1, reach + 1):
         @pl.when(s + d < seqs)
         def _():
@@ -483,6 +494,7 @@
     load_own[1].wait()
     to_sib(2).wait_recv()
     arrived(3)
+    arrived(4)
     for copy in share_pair:
         copy.wait_recv()
     for first in range(0, width, chunk):
@@ -493,10 +505,10 @@
         copy.wait_send()
     for t in range(3):
         to_sib(t).wait_send()
-    for i in range(4):
+    for i in range(5):
         for slot in (ACROSS, DIAG):
             to_far(i, slot).wait_send()
-            for step in range(3):
+            for step in steps_of(i):
                 relay(i, slot, step).wait_send()
     for d in range(1, reach + 1):
         @pl.when(s + d < seqs)
@@ -549,9 +561,12 @@
             pltpu.SemaphoreType.DMA((9,)),
         ],
         compiler_params=pltpu.CompilerParams(
-            collective_id=0, has_side_effects=True, vmem_limit_bytes=63 * 1024 * 1024,
+            collective_id=0, has_side_effects=True, vmem_limit_bytes=48 * 1024 * 1024,
         ),
-    )(query, keys, values, d_out.T, w_out, w_query, w_key, w_value).T
+    )(*(
+        pltpu.with_memory_space_constraint(x, pltpu.HBM)
+        for x in (query, keys, values, d_out.T, w_out, w_query, w_key, w_value)
+    )).T
 
 
 def solution(mesh):

time: 45.2 us -> 44 us (0.973)
  local copies, waits for them, and re-layouts: 1.99 us -> 0.85 us
    unnamed x1, local copies, waits for them, and re-layouts: 1.99 us -> 0.85 us
where the time goes in v4:
time: 44 us; the launch traced here: 43.9 us
  Pallas kernels  43 us (98%)
  local copies, waits for them, and re-layouts  0.85 us (2%)
    pallas_call x1, Pallas kernels, fused(): pl.pallas_call(functools.partial(kernel, seqs), out_shape=jax.ShapeDtypeS...  43 us

profile of v4, /device:TPU:0, one launch (start us, length us, event | category | flops | bytes accessed | tf_op | source)
XLA Modules:
  0.0 43.9 jit_solution(14426738122660064090)
XLA Ops:
  0.0 43.0 %shard_map.82 = bf16[1344,256]{1,0:T(8,128)(2,1)S(1)} custom-call(bf16[256,128]{1,0:T(8,128)(2,1)} %query_in.1, bf16[256,128]{1,0:T(8,128)(2,1)} %keys_in.1, bf16[256,128]{1,0:T(8,128)(2,1)} %values_in.1, bf16[1344,256]{1,0:T(8,128)(2,1)} %bitcast.3, bf16[128,5376]{1,0:T(8,128)(2,1)} %w_out.1, bf16[5376,128]{1,0:T(8,128)(2,1)} %w_query.1, ...), custom_call_target="tpu_custom_call" | custom-call | tf_op jit(solution)/shard_map/pallas_call | solution.py:531
  43.0 0.8 %copy.10 = bf16[256,1344]{0,1:T(8,128)(2,1)} copy(bf16[256,1344]{0,1:T(8,128)(2,1)S(1)} %bitcast.2) | data formatting | bytes 1376256

commit v5 on v4

--- a/solution.py
+++ b/solution.py
@@ -113,7 +113,7 @@
 
 def kernel(
     seqs, query_in, keys_in, values_in, d_out, w_out, w_query, w_key, w_value, out,
-    wq_all, wkv_all, wout_all, d_own, w_cut, w_heads, query, kv, probs, low, ds,
+    wq_all, wkv_all, wout_all, d_own, w_cut, w_heads, query, kv, probs, products, low, ds,
     own_part, partial, partial_in, parts, parts_in, back, back_in, grads, weights, total, acc,
     send, recv, local,
 ):
@@ -348,33 +348,25 @@
     load_query.wait()
     get_halo(0)
 
+    row = lax.broadcasted_iota(jnp.int32, (tokens, tokens), 0)
+    col = lax.broadcasted_iota(jnp.int32, (tokens, tokens), 1)
+    query_all = query[...]
+    for j in range(reach + 1):
+        score = dot_rows(query_all, kv[0, j]) * score_scale
+        if j == reach:
+            score = jnp.where(col <= row, score, -1e30)
+        else:
+            score = jnp.where(s >= reach - j, score, -1e30)
+            if j == 0:
+                score = jnp.where(col > row, score, -1e30)
+        probs[:, j * tokens : (j + 1) * tokens] = score
     for i in range(ROW_CHUNKS):
         here = pl.ds(i * rows, rows)
-        row = lax.broadcasted_iota(jnp.int32, (rows, tokens), 0) + i * rows
-        col = lax.broadcasted_iota(jnp.int32, (rows, tokens), 1)
-        scores = []
-        for j in range(reach + 1):
-            score = dot_rows(query[here, :], kv[0, j]) * score_scale
-            if j == reach:
-                score = jnp.where(col <= row, score, -1e30)
-            else:
-                score = jnp.where(s >= reach - j, score, -1e30)
-                if j == 0:
-                    score = jnp.where(col > row, score, -1e30)
-            scores.append(score)
-        top = scores[0]
-        for score in scores[1:]:
-            top = jnp.maximum(top, score)
-        top = jnp.max(top, axis=1, keepdims=True)
-        exps = [jnp.exp(score - top) for score in scores]
-        mass = exps[0]
-        for e in exps[1:]:
-            mass = mass + e
-        inverse = 1.0 / jnp.sum(mass, axis=1, keepdims=True)
-        for j in range(reach + 1):
-            p = exps[j] * inverse
-            probs[here, j * tokens : (j + 1) * tokens] = p
-            low[here, j * tokens : (j + 1) * tokens] = p.astype(bf16)
+        score = probs[here, :]
+        exps = jnp.exp(score - jnp.max(score, axis=1, keepdims=True))
+        p = exps * (1.0 / jnp.sum(exps, axis=1, keepdims=True))
+        probs[here, :] = p
+        low[here, :] = p.astype(bf16)
 
     pass_halo(1)
     relay_second(2)
@@ -418,25 +410,15 @@
                         back_copies[d - 1].start()
 
     get_halo(1)
+    for j in range(reach + 1):
+        products[:, j * tokens : (j + 1) * tokens] = dot_rows(grad_heads, kv[1, j])
+    send_back(1)
     for i in range(ROW_CHUNKS):
-        if i == ROW_CHUNKS // 2:
-            send_back(1)
         here = pl.ds(i * rows, rows)
-        block = grad_heads[i * rows : (i + 1) * rows]
-        weighted = []
-        products = []
-        for j in range(reach + 1):
-            p = probs[here, j * tokens : (j + 1) * tokens]
-            dp = dot_rows(block, kv[1, j])
-            products.append(dp)
-            weighted.append(p * dp)
-        delta = weighted[0]
-        for w in weighted[1:]:
-            delta = delta + w
-        delta = jnp.sum(delta, axis=1, keepdims=True)
-        for j in range(reach + 1):
-            p = probs[here, j * tokens : (j + 1) * tokens]
-            ds[here, j * tokens : (j + 1) * tokens] = (p * (products[j] - delta)).astype(bf16)
+        p = probs[here, :]
+        dp = products[here, :]
+        delta = jnp.sum(p * dp, axis=1, keepdims=True)
+        ds[here, :] = (p * (dp - delta)).astype(bf16)
     for j in range(reach + 1):
         parts[0, j] = (
             dot_cols(ds[:, j * tokens : (j + 1) * tokens], query[...]) * score_scale
@@ -470,16 +452,15 @@
     load_own[0].wait()
     to_sib(1).wait_recv()
     arrived(2)
-    chunk = width // 7
-
-    def product(t, first):
-        right = jnp.concatenate([grads[t, r] for r in range(PEERS)], axis=1)
-        left = jnp.concatenate(
-            [weights[t, r, first : first + chunk] for r in range(PEERS)], axis=1)
+    chunk = width // 2
+
+    def product(t, slots, first):
+        right = jnp.concatenate([grads[t, r] for r in slots], axis=1)
+        left = jnp.concatenate([weights[t, r, first : first + chunk] for r in slots], axis=1)
         return dot_rows(left, right)
 
     for first in range(0, width, chunk):
-        acc[first : first + chunk] = product(0, first)
+        acc[first : first + chunk] = product(0, range(PEERS), first)
     relay_first(4)
     for d in range(1, reach + 1):
         @pl.when(s + d < seqs)
@@ -493,13 +474,16 @@
 
     load_own[1].wait()
     to_sib(2).wait_recv()
+    share_pair[SIB - 1].wait_recv()
+    for first in range(0, width, chunk):
+        acc[first : first + chunk] += product(1, (0, SIB), first)
     arrived(3)
     arrived(4)
-    for copy in share_pair:
+    for copy in share_pair[SIB:]:
         copy.wait_recv()
     for first in range(0, width, chunk):
         here = slice(first, first + chunk)
-        out[here] = (acc[here] + product(1, first)).astype(bf16)
+        out[here] = (acc[here] + product(1, (ACROSS, DIAG), first)).astype(bf16)
 
     for copy in part + share_query + share_pair + [swap]:
         copy.wait_send()
@@ -542,6 +526,7 @@
             pltpu.VMEM((PEERS, HEAD, wide), bf16),
             pltpu.VMEM((tokens, HEAD), bf16),
             pltpu.VMEM((2, NBR + 1, tokens, HEAD), bf16),
+            pltpu.VMEM((tokens, span), f32),
             pltpu.VMEM((tokens, span), f32),
             pltpu.VMEM((tokens, span), bf16),
             pltpu.VMEM((tokens, span), bf16),
@@ -587,7 +572,7 @@
         args = (query, keys, values, d_out, w_out, w_query, w_key, w_value)
         tokens, width = d_out.shape
         fits = peers == PEERS and seqs % 4 == 0 and query.shape[1] == HEAD
-        fits = fits and tokens * NBR == WINDOW and width % (64 * 7) == 0
+        fits = fits and tokens * NBR == WINDOW and width % 64 == 0
         return fused(seqs, *args) if fits else body(*args)
 
     return jax.shard_map(local, mesh=mesh, in_specs=in_specs, out_specs=out_specs, check_vma=False)

time: 44 us -> 43.3 us (0.984)
  Pallas kernels: 43 us -> 42.3 us
    pallas_call x1, Pallas kernels: 43 us -> 42.3 us  [fused(): pl.pallas_call(functools.partial(kernel, seqs), out_shape=jax.ShapeDtypeS...]
where the time goes in v5:
time: 43.3 us; the launch traced here: 43.2 us
  Pallas kernels  42.3 us (98%)
  local copies, waits for them, and re-layouts  0.85 us (2%)
    pallas_call x1, Pallas kernels, fused(): pl.pallas_call(functools.partial(kernel, seqs), out_shape=jax.ShapeDtypeS...  42.3 us

profile of v5, /device:TPU:0, one launch (start us, length us, event | category | flops | bytes accessed | tf_op | source)
XLA Modules:
  0.0 43.2 jit_solution(2714232383008462635)
XLA Ops:
  0.0 42.3 %shard_map.82 = bf16[1344,256]{1,0:T(8,128)(2,1)S(1)} custom-call(bf16[256,128]{1,0:T(8,128)(2,1)} %query_in.1, bf16[256,128]{1,0:T(8,128)(2,1)} %keys_in.1, bf16[256,128]{1,0:T(8,128)(2,1)} %values_in.1, bf16[1344,256]{1,0:T(8,128)(2,1)} %bitcast.3, bf16[128,5376]{1,0:T(8,128)(2,1)} %w_out.1, bf16[5376,128]{1,0:T(8,128)(2,1)} %w_query.1, ...), custom_call_target="tpu_custom_call" | custom-call | tf_op jit(solution)/shard_map/pallas_call | solution.py:515
  42.3 0.8 %copy.10 = bf16[256,1344]{0,1:T(8,128)(2,1)} copy(bf16[256,1344]{0,1:T(8,128)(2,1)S(1)} %bitcast.2) | data formatting | bytes 1376256

commit v6 on v5

--- a/solution.py
+++ b/solution.py
@@ -106,7 +106,7 @@
 C_PASS = C_HALO + NBR
 C_PART = C_PASS + NBR
 C_SWAP = C_PART + 3
-C_BACK = C_SWAP + 1
+C_BACK = C_SWAP + NBR + 1
 C_GRAD = C_BACK + NBR
 C_END = C_GRAD + 6
 
@@ -380,25 +380,30 @@
         grad_heads = grad_heads + partial_in[r - 1].astype(f32)
     grad_heads = grad_heads.astype(bf16)
 
+    swaps = [
+        remote(C_SWAP + j, parts.at[1 - core, j], parts_in.at[j], s, sib) for j in range(reach + 1)
+    ]
+
+    def start_swap(which, j):
+        @pl.when(core == which)
+        def _():
+            swaps[j].start()
+
     for j in range(reach + 1):
         parts[1, j] = dot_cols(low[:, j * tokens : (j + 1) * tokens], grad_heads).astype(bf16)
-    swap = remote(C_SWAP, parts.at[1 - core], parts_in, s, sib)
-
-    @pl.when(core == 0)
-    def _():
-        swap.start()
+        start_swap(0, j)
 
     back_copies = [
         remote(C_BACK + d - 1, back.at[reach - d], back_in.at[d - 1], s - d, h)
         for d in range(1, reach + 1)
     ]
 
-    def send_back(which):
+    def send_back(which, blocks):
         @pl.when(core == which)
         def _():
-            swap.wait_recv()
-            for d in range(reach, -1, -1):
-                j = reach - d
+            for j in blocks:
+                d = reach - j
+                swaps[j].wait_recv()
                 both = parts[which, j].astype(f32) + parts_in[j].astype(f32)
                 if d == 0:
                     total[...] = both
@@ -409,10 +414,11 @@
                     def _():
                         back_copies[d - 1].start()
 
+    send_back(1, range(2))
     get_halo(1)
     for j in range(reach + 1):
         products[:, j * tokens : (j + 1) * tokens] = dot_rows(grad_heads, kv[1, j])
-    send_back(1)
+    send_back(1, range(2, reach + 1))
     for i in range(ROW_CHUNKS):
         here = pl.ds(i * rows, rows)
         p = probs[here, :]
@@ -423,10 +429,7 @@
         parts[0, j] = (
             dot_cols(ds[:, j * tokens : (j + 1) * tokens], query[...]) * score_scale
         ).astype(bf16)
-
-    @pl.when(core == 1)
-    def _():
-        swap.start()
+        start_swap(1, j)
 
     grad_query = jnp.zeros((tokens, HEAD), f32)
     for j in range(reach + 1):
@@ -434,7 +437,7 @@
             ds[:, j * tokens : (j + 1) * tokens], kv[0, j], preferred_element_type=f32)
     grads[0, 0] = (grad_query * score_scale).astype(bf16)
 
-    send_back(0)
+    send_back(0, range(reach + 1))
 
     def share(t):
         return [
@@ -485,7 +488,7 @@
         here = slice(first, first + chunk)
         out[here] = (acc[here] + product(1, (ACROSS, DIAG), first)).astype(bf16)
 
-    for copy in part + share_query + share_pair + [swap]:
+    for copy in part + share_query + share_pair + swaps:
         copy.wait_send()
     for t in range(3):
         to_sib(t).wait_send()

time: 43.3 us -> 43.4 us (level)
  no operation moved by 1% of the time
where the time goes in v6:
time: 43.4 us; the launch traced here: 43.3 us
  Pallas kernels  42.4 us (98%)
  local copies, waits for them, and re-layouts  0.85 us (2%)
    pallas_call x1, Pallas kernels, fused(): pl.pallas_call(functools.partial(kernel, seqs), out_shape=jax.ShapeDtypeS...  42.4 us

profile of v6, /device:TPU:0, one launch (start us, length us, event | category | flops | bytes accessed | tf_op | source)
XLA Modules:
  0.0 43.3 jit_solution(5455604015743568915)
XLA Ops:
  0.0 42.4 %shard_map.82 = bf16[1344,256]{1,0:T(8,128)(2,1)S(1)} custom-call(bf16[256,128]{1,0:T(8,128)(2,1)} %query_in.1, bf16[256,128]{1,0:T(8,128)(2,1)} %keys_in.1, bf16[256,128]{1,0:T(8,128)(2,1)} %values_in.1, bf16[1344,256]{1,0:T(8,128)(2,1)} %bitcast.3, bf16[128,5376]{1,0:T(8,128)(2,1)} %w_out.1, bf16[5376,128]{1,0:T(8,128)(2,1)} %w_query.1, ...), custom_call_target="tpu_custom_call" | custom-call | tf_op jit(solution)/shard_map/pallas_call | solution.py:518
  42.4 0.8 %copy.10 = bf16[256,1344]{0,1:T(8,128)(2,1)} copy(bf16[256,1344]{0,1:T(8,128)(2,1)S(1)} %bitcast.2) | data formatting | bytes 1376256

commit v7 on v5

--- a/solution.py
+++ b/solution.py
@@ -312,8 +312,9 @@
             pltpu.make_async_copy(alls[t].at[rows_own], slabs[t].at[0], local.at[6 + t]))
     relay_first(0)
     relay_first(1)
-    for slot in (ACROSS, DIAG):
-        to_far(2, slot).start()
+    for i in (2, 3, 4):
+        for slot in (ACROSS, DIAG):
+            to_far(i, slot).start()
 
     to_sib(0).wait_recv()
     rows = tokens // ROW_CHUNKS
@@ -372,9 +373,7 @@
     relay_second(2)
     for copy in part:
         copy.wait_recv()
-    for i in (3, 4):
-        for slot in (ACROSS, DIAG):
-            to_far(i, slot).start()
+    relay_first(3)
     grad_heads = own_part[...]
     for r in range(1, PEERS):
         grad_heads = grad_heads + partial_in[r - 1].astype(f32)
@@ -445,7 +444,7 @@
     share_query = share(0)
     for copy in share_query:
         copy.start()
-    relay_first(3)
+    relay_first(4)
 
     for copy in share_query:
         copy.wait_recv()
@@ -461,7 +460,6 @@
 
     for first in range(0, width, chunk):
         acc[first : first + chunk] = product(0, range(PEERS), first)
-    relay_first(4)
     for d in range(1, reach + 1):
         @pl.when(s + d < seqs)
         def _():

time: 43.3 us -> 43.1 us (level)
  the two profiles are of different devices: /device:TPU:0 before, /device:TPU:13 now
where the time goes in v7:
time: 43.1 us; the launch traced here: 43 us
  Pallas kernels  42.1 us (98%)
  local copies, waits for them, and re-layouts  0.85 us (2%)
    pallas_call x1, Pallas kernels, fused(): pl.pallas_call(functools.partial(kernel, seqs), out_shape=jax.ShapeDtypeS...  42.1 us

profile of v7, /device:TPU:13, one launch (start us, length us, event | category | flops | bytes accessed | tf_op | source)
XLA Modules:
  0.0 43.0 jit_solution(14378570078944260930)
XLA Ops:
  0.0 42.1 %shard_map.82 = bf16[1344,256]{1,0:T(8,128)(2,1)S(1)} custom-call(bf16[256,128]{1,0:T(8,128)(2,1)} %query_in.1, bf16[256,128]{1,0:T(8,128)(2,1)} %keys_in.1, bf16[256,128]{1,0:T(8,128)(2,1)} %values_in.1, bf16[1344,256]{1,0:T(8,128)(2,1)} %bitcast.3, bf16[128,5376]{1,0:T(8,128)(2,1)} %w_out.1, bf16[5376,128]{1,0:T(8,128)(2,1)} %w_query.1, ...), custom_call_target="tpu_custom_call" | custom-call | tf_op jit(solution)/shard_map/pallas_call | solution.py:513
  42.1 0.8 %copy.10 = bf16[256,1344]{0,1:T(8,128)(2,1)} copy(bf16[256,1344]{0,1:T(8,128)(2,1)S(1)} %bitcast.2) | data formatting | bytes 1376256
